TPU v7x, 32 devices: a whole 2x2x4 slice. The times are simulated.
32 devices in a mesh: group: 2 (over x), dp: 8 (over z, y), adapter: 2 (over core).
Axes of the slice: x: 2, y: 2, z: 4, core: 2. Of those that a mesh axis runs over, the one named last changes fastest.
Arguments:
- hidden_input: bfloat16 [16384, 4096], P(('group', 'dp', 'adapter')), parts along dimension 0, may hold values from -6 to 6
- output_gradient: bfloat16 [16384, 1024], P(('group', 'dp', 'adapter')), parts along dimension 0, may hold values from -0.25 to 0.25
- frozen_value_weight: bfloat16 [4096, 1024], P('dp'), may hold values from -0.09375 to 0.09375
- adapter_down_maps: bfloat16 [64, 16, 4096], P('group', None, ('dp', 'adapter')), parts along dimension 0, may hold values from -0.09375 to 0.09375
- adapter_up_maps: bfloat16 [64, 16, 1024], P('group', None, ('dp', 'adapter')), parts along dimension 0, may hold values from -1.5 to 1.5
- segment_length_quota: int32 [32, 8], P(('group', 'dp', 'adapter')), parts along dimension 0, may hold values from 1 to 256, 512 in all within a row
- segment_tenant_id: int32 [32, 8], P(('group', 'dp', 'adapter')), parts along dimension 0, may hold values from 0 to 31
- tenant_adapter_slot: int32 [64], P('group'), parts along dimension 0, may hold values from 0 to 31, each once
Outputs:
- input_gradient: bfloat16 [16384, 4096], P(('group', 'dp', 'adapter')), parts along dimension 0
- down_map_gradient: float32 [64, 16, 4096], P('group', None, ('dp', 'adapter')), parts along dimension 0
- up_map_gradient: float32 [64, 16, 1024], P('group', None, ('dp', 'adapter')), parts along dimension 0
There are 2 independent parts, one for each index of `group`. A program takes and returns all parts, laid end to end along the dimension named above; an argument that names none is the same for every part. Nothing has to cross between parts.
Inputs may be any that keep to these rules, and one draw needn't show every extreme that they name: `segment_length_quota`: each row's quotas sum to 512; some segment of each row has exactly 256 tokens. `tenant_adapter_slot`: A permutation of the slots.
All inputs are finite; a program needn't handle non-finite values.
Results may differ from a plain program's by a relative error of at most 0.0046.
Values may be sent and summed in bfloat16 or wider, within the bound.
A program may use at most 256 MiB of HBM per device.

v0:
```python
import jax
import jax.numpy as jnp
from jax import lax
from jax.sharding import PartitionSpec as P

adapter_scale = 2.0


def token_slots(segment_length_quota, segment_tenant_id, tenant_adapter_slot, tok):
    segs = segment_length_quota.shape[1]
    bounds = jnp.cumsum(segment_length_quota, axis=1)
    position = lax.iota(jnp.int32, tok)
    inside = (position[None, :, None] >= bounds[:, None, :]).astype(jnp.int32)
    seg_index = jnp.sum(inside, axis=2)
    seg_hot = (seg_index[:, :, None] == lax.iota(jnp.int32, segs)[None, None, :]).astype(jnp.int32)
    tenant = jnp.sum(seg_hot * segment_tenant_id[:, None, :], axis=2)
    segment_count = tenant_adapter_slot.shape[0]
    tenant_hot = (tenant[:, :, None] == lax.iota(jnp.int32, segment_count)[None, None, :]).astype(
        jnp.int32
    )
    slot = jnp.sum(tenant_hot * tenant_adapter_slot[None, None, :], axis=2)
    return (seg_hot, slot)


def contract_trailing(left, right):
    return lax.dot_general(
        left, right, (((1,), (1,)), ((), ())), preferred_element_type=jnp.float32
    )


def contract_leading(left, right):
    return lax.dot_general(
        left, right, (((0,), (0,)), ((), ())), preferred_element_type=jnp.float32
    )


def shards(
    hidden_input,
    output_gradient,
    frozen_value_weight,
    adapter_down_maps,
    adapter_up_maps,
    segment_length_quota,
    segment_tenant_id,
    tenant_adapter_slot,
):
    tok = hidden_input.shape[0]
    segment_count = tenant_adapter_slot.shape[0]
    adapter_rank_size = adapter_down_maps.shape[1]
    feature_width = hidden_input.shape[1]
    output_heads = output_gradient.shape[1]
    base_product = contract_trailing(
        output_gradient, lax.all_gather(frozen_value_weight, "dp", axis=0, tiled=True)
    )
    table_down, table_up = (
        lax.all_gather(adapter_down_maps, ("dp", "adapter"), axis=2, tiled=True),
        lax.all_gather(adapter_up_maps, ("dp", "adapter"), axis=2, tiled=True),
    )
    seg_hot, slot = token_slots(segment_length_quota, segment_tenant_id, tenant_adapter_slot, tok)
    seg_hot = seg_hot[0]
    slot = slot[0]
    slot_hot = (slot[:, None] == lax.iota(jnp.int32, segment_count)[None, :]).astype(jnp.float32)
    segment_mask_table = jnp.repeat(slot_hot, adapter_rank_size, axis=1)
    down_flattened = table_down.reshape(segment_count * adapter_rank_size, feature_width)
    up_flattened = table_up.reshape(segment_count * adapter_rank_size, output_heads)
    adapter_input = (contract_trailing(hidden_input, down_flattened) * segment_mask_table).astype(
        jnp.bfloat16
    )
    adapter_gradient = (
        adapter_scale * contract_trailing(output_gradient, up_flattened) * segment_mask_table
    ).astype(jnp.bfloat16)
    adapter_term = jnp.dot(adapter_gradient, down_flattened, preferred_element_type=jnp.float32)
    input_gradient = (base_product + adapter_term).astype(jnp.bfloat16)
    down_term = contract_leading(adapter_gradient, hidden_input).reshape(
        segment_count, adapter_rank_size, feature_width
    )
    up_term = (adapter_scale * contract_leading(adapter_input, output_gradient)).reshape(
        segment_count, adapter_rank_size, output_heads
    )
    down_map_gradient, up_map_gradient = (
        lax.psum_scatter(down_term, ("dp", "adapter"), scatter_dimension=2, tiled=True),
        lax.psum_scatter(up_term, ("dp", "adapter"), scatter_dimension=2, tiled=True),
    )
    return (input_gradient, down_map_gradient, up_map_gradient)


def solution(mesh):
    return jax.shard_map(
        shards,
        mesh=mesh,
        in_specs=(
            P(("group", "dp", "adapter"), None),
            P(("group", "dp", "adapter"), None),
            P("dp", None),
            P("group", None, ("dp", "adapter")),
            P("group", None, ("dp", "adapter")),
            P(("group", "dp", "adapter"), None),
            P(("group", "dp", "adapter"), None),
            P("group"),
        ),
        out_specs=(
            P(("group", "dp", "adapter"), None),
            P("group", None, ("dp", "adapter")),
            P("group", None, ("dp", "adapter")),
        ),
        check_vma=False,
    )
```

profile of v0, /device:TPU:13, one launch (start us, length us, event | category | flops | bytes accessed | tf_op | source)
XLA Modules:
  0.0 421.4 jit_solution(7818773034443889537)
XLA Ops:
  7.2 0.0 copy-start
  7.2 0.0 all-gather.8.cloned.1.call-start
  7.2 0.7 all-gather.8.cloned.1.call-update
  7.9 0.0 all-gather.6.cloned.1.call-start
  8.0 1.9 copy.19
  9.9 0.0 all-gather.6.cloned.1.call-update
  9.9 0.0 reduce-scatter.7.cloned.1.call-start
  9.9 0.8 reduce_window_sum.11
  10.8 0.1 convert_reduce_fusion
  10.8 0.7 select_reduce_fusion.1
  11.6 0.7 select_reduce_fusion
  12.3 0.1 broadcast_in_dim.2
  12.5 0.3 copy.21
  12.8 0.0 copy-start.1
  12.8 49.5 %all-gather.8.cloned.1.call-done = bf16[32,16,4096]{2,1,0:T(8,128)(2,1)} async-done(((bf16[32,16,256]{2,1,0:T(8,128)(2,1)}), bf16[32,16,4096]{2,1,0:T(8,128)(2,1)}) %all-gather.8.cloned.1.call-update) | async-done | bytes 4194320 | tf_op jit(solution)/shard_map/all_gather | solution.py:56
  62.3 0.0 copy-done
  62.3 7.8 %convolution_multiply_fusion = f32[512,1024]{1,0:T(8,128)} fusion(bf16[512,1024]{1,0:T(8,128)(2,1)S(1)} %copy-done, f32[512,512]{1,0:T(8,128)S(1)} %copy.21, bf16[512,4096]{1,0:T(8,128)(2,1)} %param.8, bf16[512,4096]{1,0:T(8,128)(2,1)} %bitcast.25), kind=kOutput, calls=%fused_computation.1 | convolution fusion | flops 2685403136 | bytes 12582912 | tf_op jit(solution)/shard_map/dot_general | solution.py:32
  70.1 0.0 copy-done.1
  70.1 14.3 %copy.23 = f32[32,16,1024]{1,0,2:T(8,128)} copy(f32[32,16,1024]{2,1,0:T(8,128)} %bitcast.27) | data formatting | bytes 4194304
  84.3 15.1 %reshape.202 = f32[1024,512]{1,0:T(8,128)} reshape(f32[1024,32,16]{2,1,0:T(8,128)} %bitcast.20) | data formatting | bytes 4194304
  99.5 0.0 reduce-scatter.7.cloned.1.call-update
  99.5 0.0 all-gather.4.cloned.1.call-start
  99.6 0.5 all-gather.4.cloned.1.call-update
  100.1 0.2 reduce-scatter.5.cloned.1.call-start
  100.3 15.4 %all-gather.6.cloned.1.call-done = bf16[32,16,1024]{0,1,2:T(8,128)(2,1)} async-done(((bf16[32,16,64]{0,1,2:T(8,128)(2,1)}), bf16[32,16,1024]{0,1,2:T(8,128)(2,1)}) %all-gather.6.cloned.1.call-update) | async-done | bytes 1048592 | tf_op jit(solution)/shard_map/all_gather | solution.py:57
  115.7 5.2 %copy.20 = bf16[32,16,1024]{2,1,0:T(8,128)(2,1)S(1)} copy(bf16[32,16,1024]{0,1,2:T(8,128)(2,1)} %all-gather.6.cloned.1.call-done) | data formatting | bytes 2097152 | tf_op jit(solution)/shard_map/all_gather | solution.py:57
  121.0 2.0 fusion.2
  122.9 7.8 %fusion.5 = f32[512,4096]{1,0:T(8,128)} fusion(bf16[512,512]{1,0:T(8,128)(2,1)S(1)} %fusion.2, bf16[512,4096]{1,0:T(8,128)(2,1)} %param.8), kind=kOutput, calls=%fused_computation.16 | convolution fusion | flops 2147483648 | bytes 13107200 | tf_op jit(solution)/shard_map/dot_general | solution.py:32
  130.7 0.0 reduce-scatter.5.cloned.1.call-update
  130.7 47.9 %reduce-scatter.7.cloned.1.call-done = f32[64,512]{1,0:T(8,128)} async-done(((f32[1024,512]{1,0:T(8,128)}), f32[64,512]{1,0:T(8,128)}) %reduce-scatter.7.cloned.1.call-update) | async-done | bytes 131088
  178.6 1.3 reshape.203
  179.9 1.3 copy.24
  181.2 122.5 %all-gather.4.cloned.1.call-done = bf16[4096,1024]{1,0:T(8,128)(2,1)} async-done(((bf16[512,1024]{1,0:T(8,128)(2,1)}), bf16[4096,1024]{1,0:T(8,128)(2,1)}) %all-gather.4.cloned.1.call-update) | async-done | bytes 8388624 | tf_op jit(solution)/shard_map/all_gather | solution.py:53
  303.7 0.0 copy-start.2
  303.7 7.1 %fusion.4 = f32[512,4096]{1,0:T(8,128)S(1)} fusion(bf16[512,1024]{1,0:T(8,128)(2,1)S(1)} %copy-done, bf16[4096,1024]{1,0:T(8,128)(2,1)} %all-gather.4.cloned.1.call-done), kind=kOutput, calls=%fused_computation.15 | convolution fusion | flops 4294967296 | bytes 17825792 | tf_op jit(solution)/shard_map/dot_general | solution.py:26
  310.8 0.0 copy-done.2
  310.8 4.5 %add_convert_fusion = bf16[512,4096]{1,0:T(8,128)(2,1)} fusion(f32[512,4096]{1,0:T(8,128)S(1)} %fusion.4, bf16[512,512]{1,0:T(8,128)(2,1)S(1)} %fusion.2, bf16[512,4096]{1,0:T(8,128)(2,1)S(1)} %bitcast.26), kind=kOutput, calls=%fused_computation | convolution fusion | flops 2151677952 | bytes 17301504 | tf_op jit(solution)/shard_map/dot_general | solution.py:72
  315.3 99.6 %reduce-scatter.5.cloned.1.call-done = f32[32,16,256]{2,1,0:T(8,128)} async-done(((f32[32,16,4096]{2,1,0:T(8,128)}), f32[32,16,256]{2,1,0:T(8,128)}) %reduce-scatter.5.cloned.1.call-update) | async-done | bytes 524304 | tf_op jit(solution)/shard_map/reduce_scatter | solution.py:81
  (1 shorter events, 0.0 us)
Async XLA Ops:
  7.2 55.1 %copy-start = (bf16[512,1024]{1,0:T(8,128)(2,1)S(1)}, bf16[512,1024]{1,0:T(8,128)(2,1)}, u32[]{:S(2)}) copy-start(bf16[512,1024]{1,0:T(8,128)(2,1)} %param.9) | copy-start | bytes 3145732
  7.2 55.1 %all-gather.8.cloned.1.call-start = ((), (), s32[]{:S(2)}) async-start(), calls=%async_computation.4 | async-start | bytes 4456448 | tf_op jit(solution)/shard_map/all_gather | solution.py:56
  7.9 107.8 %all-gather.6.cloned.1.call-start = ((), (), s32[]{:S(2)}) async-start(), calls=%async_computation.3 | async-start | bytes 4456448 | tf_op jit(solution)/shard_map/all_gather | solution.py:57
  9.9 168.7 %reduce-scatter.7.cloned.1.call-start = ((), (), s32[]{:S(2)}) async-start(), calls=%async_computation.6 | async-start | bytes 2228224
  12.8 57.3 %copy-start.1 = (f32[512,512]{1,0:T(8,128)}, f32[512,512]{1,0:T(8,128)S(1)}, u32[]{:S(2)}) copy-start(f32[512,512]{1,0:T(8,128)S(1)} %copy.21) | copy-start | bytes 3145732
  99.5 204.2 %all-gather.4.cloned.1.call-start = ((), (), s32[]{:S(2)}) async-start(), calls=%async_computation.2 | async-start | bytes 9437184 | tf_op jit(solution)/shard_map/all_gather | solution.py:53
  100.1 314.8 %reduce-scatter.5.cloned.1.call-start = ((), (), s32[]{:S(2)}) async-start(), calls=%async_computation.5 | async-start | bytes 8912896 | tf_op jit(solution)/shard_map/reduce_scatter | solution.py:81
  303.7 7.1 %copy-start.2 = (bf16[32,16,4096]{2,1,0:T(8,128)(2,1)S(1)}, bf16[32,16,4096]{2,1,0:T(8,128)(2,1)}, u32[]{:S(2)}) copy-start(bf16[32,16,4096]{2,1,0:T(8,128)(2,1)} %all-gather.8.cloned.1.call-done) | copy-start | bytes 12582916
Sparse Core Ops, SparseCore 0:
  10.2 52.0 all-gather.7
  65.0 50.6 all-gather.5
  120.0 58.5 reduce-scatter.6
  180.8 122.8 all-gather.3
  308.8 106.1 reduce-scatter.4
where the time goes:
time: 424 us; the launch traced here: 421 us
  waiting for transfers between devices  336 us (79%)
  local copies, waits for them, and re-layouts  39.6 us (9%)
  matrix products  29.2 us (7%)
  between operations  13.9 us (3%)
    all_gather x1, waiting for transfers between devices, shards(): lax.all_gather(frozen_value_weight, 'dp', axis=0, tiled=True)  123 us
    reduce_scatter x1, waiting for transfers between devices, shards(): lax.psum_scatter(down_term, ('dp', 'adapter'), scatter_dimension=2, tiled...  99.6 us
    all_gather x1, waiting for transfers between devices, shards(): lax.all_gather(adapter_down_maps, ('dp', 'adapter'), axis=2, tiled=True)  49.5 us
    unnamed x6, waiting for transfers between devices  49.1 us
    unnamed x11, local copies, waits for them, and re-layouts  33.9 us
    dot_general x2, matrix products, contract_leading(): lax.dot_general(left, right, (((0,), (0,)), ((), ())), preferred_element_...  15.6 us
    all_gather x1, waiting for transfers between devices, shards(): lax.all_gather(adapter_up_maps, ('dp', 'adapter'), axis=2, tiled=True)  15.4 us
    dot_general x2, matrix products, contract_trailing(): lax.dot_general(left, right, (((1,), (1,)), ((), ())), preferred_element_...  9.08 us
  transfers between devices with their start and end apart: 5, of which 5 were waited for; matrix products, arithmetic and copies ran while one was open for 17% of the time, Pallas kernels for 0%

commit v1 on v0

v1 whole, which is shorter than its diff:
```python
import functools

import jax
import jax.numpy as jnp
from jax import lax
from jax.experimental import pallas as pl
from jax.experimental.pallas import tpu as pltpu
from jax.sharding import PartitionSpec as P

adapter_scale = 2.0
MESH = pl.DeviceIdType.MESH


def ring_position(d, n):
    odd = lax.rem(d, 2)
    half = lax.div(d, 2)
    return (1 - odd) * half + odd * (n - 1 - half)


def ring_device(p, n):
    p = lax.rem(p + n, n)
    upper = lax.div(p, n // 2)
    return (1 - upper) * (2 * p) + upper * (2 * (n - 1 - p) + 1)


class Ring:
    def __init__(self, n, items, sems):
        self.n, self.items = n, items
        self.ring_send, self.ring_recv, self.side_send, self.side_recv, self.local = sems
        self.me = lax.axis_index("dp")
        self.lane = lax.axis_index("adapter")
        self.pos = ring_position(self.me, n)
        self.right = ring_device(self.pos + 1, n)
        self.left = ring_device(self.pos + n - 1, n)
        self.steps = n // 2
        self.copies = {}
        self.sides = []
        self.locals = []

    def window(self, item, device, step, way):
        rows = item[2]
        if step < self.steps - 1:
            return 0, rows
        if rows % 32 == 0:
            return (0, rows // 2) if way == 0 else (rows // 2, rows // 2)
        return (0, rows) if way == 0 else (0, 0)

    def target_rows(self, item, device, lane, start, count):
        rows = item[2]
        return item[1].at[pl.ds(pl.multiple_of((device * 2 + lane) * rows + start, 16), count)]

    def begin(self):
        for i, item in enumerate(self.items):
            source, target, rows, shared = item
            if shared:
                own = pltpu.make_async_copy(
                    source, target.at[pl.ds(pl.multiple_of(self.me * 2 * rows, 16), 2 * rows)], self.local.at[i]
                )
            else:
                own = pltpu.make_async_copy(
                    source, self.target_rows(item, self.me, self.lane, 0, rows), self.local.at[i]
                )
            own.start()
            self.locals.append(own)
        for i in range(len(self.items)):
            self.send(i, 0)
        for i, item in enumerate(self.items):
            if not item[3]:
                self.side(i, item[0], self.me, 0, item[2], 0)

    def send(self, i, step):
        item = self.items[i]
        for way in (0, 1):
            start, count = self.window(item, None, step, way)
            if count == 0:
                continue
            back = self.n - step if way == 0 else step
            device = ring_device(self.pos + back, self.n)
            target = self.target_rows(item, device, self.lane, start, count)
            if step == 0:
                base = pl.multiple_of(self.lane * item[2] + start, 16) if item[3] else start
                source = item[0].at[pl.ds(base, count)]
            else:
                source = target
            copy = pltpu.make_async_remote_copy(
                src_ref=source,
                dst_ref=target,
                send_sem=self.ring_send.at[i, way, step],
                recv_sem=self.ring_recv.at[i, way, step],
                device_id={"dp": self.right if way == 0 else self.left},
                device_id_type=MESH,
            )
            copy.start()
            self.copies[i, way, step] = copy

    def side(self, i, source, device, start, count, slot):
        item = self.items[i]
        copy = pltpu.make_async_remote_copy(
            src_ref=source,
            dst_ref=self.target_rows(item, device, self.lane, start, count),
            send_sem=self.side_send.at[i, slot],
            recv_sem=self.side_recv.at[i, slot],
            device_id={"adapter": 1 - self.lane},
            device_id_type=MESH,
        )
        copy.start()
        self.sides.append(copy)

    def run(self):
        for step in range(self.steps):
            for i, item in enumerate(self.items):
                for way in (0, 1):
                    if (i, way, step) in self.copies:
                        self.copies[i, way, step].wait_recv()
                if step + 1 < self.steps:
                    self.send(i, step + 1)
                for way in (0, 1):
                    start, count = self.window(item, None, step, way)
                    if count == 0:
                        continue
                    ahead = self.n - 1 - step if way == 0 else 1 + step
                    device = ring_device(self.pos + ahead, self.n)
                    block = self.target_rows(item, device, self.lane, start, count)
                    self.side(i, block, device, start, count, 1 + 2 * step + way)

    def finish(self):
        for copy in self.copies.values():
            copy.wait_send()
        for copy in self.sides:
            copy.wait()
        for copy in self.locals:
            copy.wait()


def ring_scratch(n, items):
    return [
        pltpu.SemaphoreType.DMA((items, 2, n // 2)),
        pltpu.SemaphoreType.DMA((items, 2, n // 2)),
        pltpu.SemaphoreType.DMA((items, 1 + n)),
        pltpu.SemaphoreType.DMA((items, 1 + n)),
        pltpu.SemaphoreType.DMA((items,)),
    ]


def greet_ring(barrier, n):
    lane, pos = lax.axis_index("adapter"), ring_position(lax.axis_index("dp"), n)
    for device in (ring_device(pos + 1, n), ring_device(pos + n - 1, n)):
        pl.semaphore_signal(barrier, inc=1, device_id={"dp": device}, device_id_type=MESH)
    pl.semaphore_signal(barrier, inc=1, device_id={"adapter": 1 - lane}, device_id_type=MESH)
    pl.semaphore_wait(barrier, 3)


def maps_kernel(n, down_ref, up_ref, down_out, up_out, *sems):
    greet_ring(pltpu.get_barrier_semaphore(), n)
    ring = Ring(n, [(down_ref, down_out, down_ref.shape[0], False), (up_ref, up_out, up_ref.shape[0], False)], sems)
    ring.begin()
    ring.run()
    ring.finish()


def weight_kernel(n, weight_ref, down_ref, up_ref, hot_ref, weight_out, down_out, up_out, hot_out, *sems):
    devices = 2 * n
    ring_sems, (send_sem, recv_sem, local_sem) = sems[:5], sems[5:]
    me = lax.axis_index("dp") * 2 + lax.axis_index("adapter")
    barrier = pltpu.get_barrier_semaphore()

    def peer_of(k):
        peer = lax.rem(me + k, devices)
        return {"dp": lax.div(peer, 2), "adapter": lax.rem(peer, 2)}, peer

    def greet(k, carry):
        pl.semaphore_signal(barrier, inc=1, device_id=peer_of(k)[0], device_id_type=MESH)
        return carry

    lax.fori_loop(1, devices, greet, 0)
    pl.semaphore_wait(barrier, devices - 1)

    rows_down, rows_up = down_out.shape[0], up_out.shape[0]
    wide = down_ref.shape[1]

    def parts(owner, sender):
        place = pl.ds(pl.multiple_of(sender * wide, 128), wide)
        return (
            (down_ref.at[pl.ds(pl.multiple_of(owner * rows_down, 16), rows_down)], down_out.at[:, place]),
            (up_ref.at[pl.ds(pl.multiple_of(owner * rows_up, 16), rows_up)], up_out.at[:, place]),
            (hot_ref, hot_out.at[sender]),
        )

    def copies(k):
        device, peer = peer_of(k)
        return [
            pltpu.make_async_remote_copy(
                src_ref=source,
                dst_ref=target,
                send_sem=send_sem.at[i, k],
                recv_sem=recv_sem.at[i, k],
                device_id=device,
                device_id_type=MESH,
            )
            for i, (source, target) in enumerate(parts(peer, me))
        ]

    ring = Ring(n, [(weight_ref, weight_out, weight_ref.shape[0] // 2, True)], ring_sems)

    def start(k, carry):
        for copy in copies(k):
            copy.start()
        return carry

    own = [
        pltpu.make_async_copy(source, target, local_sem.at[i]) for i, (source, target) in enumerate(parts(me, me))
    ]
    for copy in own:
        copy.start()
    ring.begin()
    lax.fori_loop(1, devices, start, 0)
    ring.run()
    ring.finish()

    def end(k, carry):
        for copy in copies(k):
            copy.wait()
        return carry

    lax.fori_loop(1, devices, end, 0)
    for copy in own:
        copy.wait()


def call(kernel, outs, operands, scratch, collective_id):
    anywhere = pl.BlockSpec(memory_space=pl.ANY)
    return pl.pallas_call(
        kernel,
        out_shape=outs,
        in_specs=[anywhere] * len(operands),
        out_specs=[anywhere] * len(outs),
        scratch_shapes=scratch,
        compiler_params=pltpu.CompilerParams(collective_id=collective_id, has_side_effects=True),
    )(*operands)


def token_slots(segment_length_quota, segment_tenant_id, tenant_adapter_slot, tok):
    ends = jnp.cumsum(segment_length_quota[0])
    starts = ends - segment_length_quota[0]
    position = lax.iota(jnp.int32, tok)[:, None]
    seg_hot = (position >= starts[None, :]) & (position < ends[None, :])
    count = tenant_adapter_slot.shape[0]
    tenant_hot = segment_tenant_id[0][:, None] == lax.iota(jnp.int32, count)[None, :]
    slot = jnp.sum(tenant_hot.astype(jnp.int32) * tenant_adapter_slot[None, :], axis=1)
    return seg_hot, slot


def dot(left, right, left_dim, right_dim):
    return lax.dot_general(
        left, right, (((left_dim,), (right_dim,)), ((), ())), preferred_element_type=jnp.float32
    )


def shards(
    n,
    hidden_input,
    output_gradient,
    frozen_value_weight,
    adapter_down_maps,
    adapter_up_maps,
    segment_length_quota,
    segment_tenant_id,
    tenant_adapter_slot,
):
    tok, width = hidden_input.shape
    outputs = output_gradient.shape[1]
    slots, rank, down_columns = adapter_down_maps.shape
    up_columns = adapter_up_maps.shape[2]
    segs = segment_length_quota.shape[1]
    flat, wide, devices = slots * rank, segs * rank, 2 * n
    bf16 = jnp.bfloat16

    down_own = adapter_down_maps.reshape(flat, down_columns).T
    up_own = adapter_up_maps.reshape(flat, up_columns).T
    down, up = call(
        functools.partial(maps_kernel, n),
        [jax.ShapeDtypeStruct((width, flat), bf16), jax.ShapeDtypeStruct((outputs, flat), bf16)],
        [down_own, up_own],
        ring_scratch(n, 2),
        0,
    )

    seg_hot, slot = token_slots(segment_length_quota, segment_tenant_id, tenant_adapter_slot, tok)
    slot_hot = slot[:, None] == lax.iota(jnp.int32, slots)[None, :]
    seg_mask = jnp.repeat(seg_hot.astype(jnp.float32), rank, axis=1)
    token_hot = dot(seg_hot.astype(bf16), slot_hot.astype(bf16), 1, 0)
    mask = jnp.repeat(token_hot, rank, axis=1)
    fold = (
        lax.rem(lax.iota(jnp.int32, flat), rank)[:, None] == lax.rem(lax.iota(jnp.int32, wide), rank)[None, :]
    ).astype(bf16)

    lora_in = (dot(hidden_input, down, 1, 0) * mask).astype(bf16)
    lora_grad = (adapter_scale * dot(output_gradient, up, 1, 0) * mask).astype(bf16)
    lora_in_seg = (dot(lora_in, fold, 1, 0) * seg_mask).astype(bf16)
    lora_grad_seg = (dot(lora_grad, fold, 1, 0) * seg_mask).astype(bf16)
    down_term = dot(hidden_input, lora_grad_seg, 0, 0).astype(bf16)
    up_term = (adapter_scale * dot(output_gradient, lora_in_seg, 0, 0)).astype(bf16)

    hot = jnp.pad(slot_hot.astype(bf16), ((0, 16 - segs % 16), (0, 128 - slots % 128)))
    weight, down_parts, up_parts, hots = call(
        functools.partial(weight_kernel, n),
        [
            jax.ShapeDtypeStruct((width, outputs), bf16),
            jax.ShapeDtypeStruct((down_columns, devices * wide), bf16),
            jax.ShapeDtypeStruct((up_columns, devices * wide), bf16),
            jax.ShapeDtypeStruct((devices,) + hot.shape, bf16),
        ],
        [frozen_value_weight, down_term, up_term, hot],
        ring_scratch(n, 1)
        + [pltpu.SemaphoreType.DMA((3, devices)), pltpu.SemaphoreType.DMA((3, devices)), pltpu.SemaphoreType.DMA((3,))],
        1,
    )

    spread = jnp.repeat(jnp.repeat(hots[:, :segs, :slots].reshape(devices * segs, slots), rank, axis=0), rank, axis=1)
    same_rank = (
        lax.rem(lax.iota(jnp.int32, devices * wide), rank)[:, None]
        == lax.rem(lax.iota(jnp.int32, flat), rank)[None, :]
    )
    spread = jnp.where(same_rank, spread, jnp.zeros_like(spread))
    down_map_gradient = dot(spread, down_parts, 0, 1).reshape(slots, rank, down_columns)
    up_map_gradient = dot(spread, up_parts, 0, 1).reshape(slots, rank, up_columns)

    input_gradient = (dot(output_gradient, weight, 1, 1) + dot(lora_grad, down, 1, 1)).astype(bf16)
    return (input_gradient, down_map_gradient, up_map_gradient)


def solution(mesh):
    return jax.shard_map(
        functools.partial(shards, mesh.shape["dp"]),
        mesh=mesh,
        in_specs=(
            P(("group", "dp", "adapter"), None),
            P(("group", "dp", "adapter"), None),
            P("dp", None),
            P("group", None, ("dp", "adapter")),
            P("group", None, ("dp", "adapter")),
            P(("group", "dp", "adapter"), None),
            P(("group", "dp", "adapter"), None),
            P("group"),
        ),
        out_specs=(
            P(("group", "dp", "adapter"), None),
            P("group", None, ("dp", "adapter")),
            P("group", None, ("dp", "adapter")),
        ),
        check_vma=False,
    )
```

time: 424 us -> 158 us (0.37)
  waiting for transfers between devices: 336 us -> 0 us
  Pallas kernels: 0 us -> 112 us
  local copies, waits for them, and re-layouts: 39.6 us -> 11 us
  between operations: 13.9 us -> 0.76 us
    all_gather x3 -> x0, waiting for transfers between devices: 187 us -> none  [the longest x1 123 us: shards(): lax.all_gather(frozen_value_weight, 'dp', axis=0, tiled=True)]
    pallas_call x0 -> x2, Pallas kernels: none -> 112 us  [call(): pl.pallas_call(kernel, out_shape=outs, in_specs=[anywhere] * len(operands...]
    reduce_scatter x1 -> x0, waiting for transfers between devices: 99.6 us -> none  [shards(): lax.psum_scatter(down_term, ('dp', 'adapter'), scatter_dimension=2, tiled...]
    unnamed x6 -> x0, waiting for transfers between devices: 49.1 us -> none
    unnamed x11, local copies, waits for them, and re-layouts: 33.9 us -> 6.36 us
    all_gather x1 -> x0, local copies, waits for them, and re-layouts: 5.24 us -> none  [shards(): lax.all_gather(adapter_up_maps, ('dp', 'adapter'), axis=2, tiled=True)]
    dot_general x5 -> x9, matrix products: 29.2 us -> 28.3 us  [dot(): lax.dot_general(left, right, (((left_dim,), (right_dim,)), ((), ())), pre...]
  transfers between devices with their start and end apart: 5 -> 0, of which waited for: 5 -> 0; matrix products, arithmetic and copies ran while one was open for 17% -> 0% of each run, Pallas kernels for 0% -> 0%
where the time goes in v1:
time: 158 us; the launch traced here: 156 us
  Pallas kernels  112 us (71%)
  matrix products  28.3 us (18%)
  local copies, waits for them, and re-layouts  11 us (7%)
  other arithmetic  3.81 us (2%)
    pallas_call x2, Pallas kernels, call(): pl.pallas_call(kernel, out_shape=outs, in_specs=[anywhere] * len(operands...  112 us
    dot_general x9, matrix products, dot(): lax.dot_general(left, right, (((left_dim,), (right_dim,)), ((), ())), pre...  28.3 us
    unnamed x11, local copies, waits for them, and re-layouts  6.36 us

profile of v1, /device:TPU:13, one launch (start us, length us, event | category | flops | bytes accessed | tf_op | source)
XLA Modules:
  0.0 155.6 jit_solution(5596337155725686023)
XLA Ops:
  0.6 0.0 copy-start
  0.6 0.9 reduce-window.4
  1.6 0.7 fusion.31
  2.2 0.9 select_reduce_fusion
  3.1 0.3 fusion.27
  3.3 1.8 %copy.25 = bf16[512,256]{0,1:T(8,128)(2,1)} copy(bf16[512,256]{1,0:T(8,128)(2,1)} %bitcast.75) | data formatting | bytes 524288 | tf_op jit(solution)/shard_map/reshape | solution.py:278
  5.1 1.6 %copy.26 = bf16[512,64]{0,1:T(8,128)(2,1)} copy(bf16[512,64]{1,0:T(8,128)(2,1)} %bitcast.76) | data formatting | bytes 131072 | tf_op jit(solution)/shard_map/reshape | solution.py:279
  6.8 31.3 %shard_map.103 = (bf16[4096,512]{1,0:T(8,128)(2,1)}, bf16[1024,512]{1,0:T(8,128)(2,1)}) custom-call(bf16[256,512]{1,0:T(8,128)(2,1)} %bitcast.72, bf16[64,512]{1,0:T(8,128)(2,1)} %bitcast.74), custom_call_target="tpu_custom_call" | custom-call | tf_op jit(solution)/shard_map/pallas_call | solution.py:232
  38.0 0.0 copy-done
  38.1 2.0 %fusion.4 = bf16[512,512]{0,1:T(8,128)(2,1)S(1)} fusion(bf16[1024,512]{1,0:T(8,128)(2,1)} %get-tuple-element.9, bf16[512,1024]{1,0:T(8,128)(2,1)S(1)} %copy-done, f32[512,32]{0,1:T(8,128)S(1)} %fusion.27), kind=kOutput, calls=%fused_computation.11 | convolution fusion | flops 537657344 | bytes 2686976 | tf_op jit(solution)/shard_map/dot_general | solution.py:254
  40.0 0.1 fusion.26
  40.1 0.1 copy.27
  40.3 5.2 %fusion.1.down_ref = bf16[4096,128]{1,0:T(8,128)(2,1)} fusion(bf16[512,4096]{1,0:T(8,128)(2,1)} %param.8, f32[512,128]{1,0:T(8,128)S(1)} %copy.27, bf16[512,512]{0,1:T(8,128)(2,1)S(1)} %fusion.4, s32[128]{0:T(128)S(1)} %iota_and_fusion.2, s32[512]{0:T(512)S(1)} %iota_and_fusion.1), kind=kOutput, calls=%fused_computation.3 | convolution fusion | flops 604700672 | bytes 6031872 | tf_op jit(solution)/shard_map/dot_general | solution.py:254
  45.5 5.8 %fusion.3 = bf16[512,512]{0,1:T(8,128)(2,1)S(1)} fusion(bf16[4096,512]{1,0:T(8,128)(2,1)} %get-tuple-element.10, bf16[512,4096]{1,0:T(8,128)(2,1)} %param.8, f32[512,32]{0,1:T(8,128)S(1)} %fusion.27), kind=kOutput, calls=%fused_computation.10 | convolution fusion | flops 2148007936 | bytes 8978432 | tf_op jit(solution)/shard_map/dot_general | solution.py:254
  51.3 1.7 %fusion.6.up_ref = bf16[1024,128]{1,0:T(8,128)(2,1)} fusion(bf16[512,1024]{1,0:T(8,128)(2,1)S(1)} %copy-done, f32[512,128]{1,0:T(8,128)S(1)} %copy.27, bf16[512,512]{0,1:T(8,128)(2,1)S(1)} %fusion.3, s32[128]{0:T(128)S(1)} %iota_and_fusion.2, s32[512]{0:T(512)S(1)} %iota_and_fusion.1), kind=kOutput, calls=%fused_computation.16 | convolution fusion | flops 201785344 | bytes 2099712 | tf_op jit(solution)/shard_map/dot_general | solution.py:254
  53.0 0.1 iota_compare_fusion.2
  53.1 0.6 pad_convert_fusion.hot_ref
  53.7 80.5 %shard_map.104 = (bf16[4096,1024]{1,0:T(8,128)(2,1)}, bf16[256,2048]{1,0:T(8,128)(2,1)}, bf16[64,2048]{1,0:T(8,128)(2,1)}, bf16[16,16,128]{2,1,0:T(8,128)(2,1)}) custom-call(bf16[512,1024]{1,0:T(8,128)(2,1)} %weight_ref.1, bf16[4096,128]{1,0:T(8,128)(2,1)} %fusion.1.down_ref, bf16[1024,128]{1,0:T(8,128)(2,1)} %fusion.6.up_ref, ...), custom_call_target="tpu_custom_call" | custom-call | tf_op jit(solution)/shard_map/pallas_call | solution.py:232
  134.1 0.0 copy-start.2
  134.1 0.8 slice_bitcast_fusion
  135.0 0.1 broadcast_in_dim.12
  135.1 0.2 copy.32
  135.3 0.0 copy-start.1
  135.3 0.6 compare_select_fusion
  135.9 2.6 %fusion.15 = f32[32,16,64]{2,1,0:T(8,128)} fusion(bf16[32,16,2048]{2,1,0:T(8,128)(2,1)S(1)} %bitcast.69, bf16[64,2048]{1,0:T(8,128)(2,1)} %get-tuple-element.14), kind=kOutput, calls=%fused_computation.23 | convolution fusion | flops 134217728 | bytes 2490368 | tf_op jit(solution)/shard_map/dot_general | solution.py:254
  138.6 0.0 copy-done.2
  138.6 0.0 slice-start
  138.6 1.6 %fusion.9 = f32[32,16,256]{2,1,0:T(8,128)} fusion(bf16[32,16,2048]{2,1,0:T(8,128)(2,1)S(1)} %bitcast.70, bf16[256,2048]{1,0:T(8,128)(2,1)S(1)} %copy-done.2), kind=kOutput, calls=%fused_computation.19 | convolution fusion | flops 536870912 | bytes 3670016 | tf_op jit(solution)/shard_map/dot_general | solution.py:254
  140.2 0.0 copy-done.1
  140.2 0.0 slice-start.1
  140.2 2.3 %fusion.32 = f32[512,4096]{0,1:T(8,128)S(1)} fusion(bf16[4096,512]{1,0:T(8,128)(2,1)S(1)} %copy-done.1, bf16[512,512]{0,1:T(8,128)(2,1)S(1)} %fusion.4), kind=kOutput, calls=%fused_computation.46 | convolution fusion | flops 2147483648 | bytes 13107200 | tf_op jit(solution)/shard_map/dot_general | solution.py:254
  142.5 0.0 slice-done
  142.5 0.0 slice-done.1
  142.6 6.8 %fusion = bf16[512,4096]{0,1:T(8,128)(2,1)} fusion(f32[512,4096]{0,1:T(8,128)S(1)} %fusion.32, bf16[4096,1024]{1,0:T(8,128)(2,1)S(1)} %bitcast.80, bf16[512,1024]{1,0:T(8,128)(2,1)S(1)} %copy-done), kind=kOutput, calls=%fused_computation.1 | convolution fusion | flops 4299161600 | bytes 22020096 | tf_op jit(solution)/shard_map/dot_general | solution.py:254
  149.3 6.3 %copy.33 = bf16[512,4096]{1,0:T(8,128)(2,1)} copy(bf16[512,4096]{0,1:T(8,128)(2,1)} %fusion) | data formatting | bytes 8388608
  (5 shorter events, 0.0 us)
Async XLA Ops:
  0.6 37.4 %copy-start = (bf16[512,1024]{1,0:T(8,128)(2,1)S(1)}, bf16[512,1024]{1,0:T(8,128)(2,1)}, u32[]{:S(2)}) copy-start(bf16[512,1024]{1,0:T(8,128)(2,1)} %param.9) | copy-start | bytes 3145732
  134.1 4.4 %copy-start.2 = (bf16[256,2048]{1,0:T(8,128)(2,1)S(1)}, bf16[256,2048]{1,0:T(8,128)(2,1)}, u32[]{:S(2)}) copy-start(bf16[256,2048]{1,0:T(8,128)(2,1)} %get-tuple-element.13) | copy-start | bytes 3145732
  135.3 4.9 %copy-start.1 = (bf16[4096,512]{1,0:T(8,128)(2,1)S(1)}, bf16[4096,512]{1,0:T(8,128)(2,1)}, u32[]{:S(2)}) copy-start(bf16[4096,512]{1,0:T(8,128)(2,1)} %get-tuple-element.10) | copy-start | bytes 12582916
  138.6 4.0 %slice-start = ((s8[8388608]{0:T(1024)(128)(4,1)}), s8[4194304]{0:T(1024)(128)(4,1)S(1)}, s32[]{:S(2)}) async-start(s8[8388608]{0:T(1024)(128)(4,1)} %bitcast.79), calls=%async_computation | async-start | bytes 8388608
  140.2 2.4 %slice-start.1 = ((s8[8388608]{0:T(1024)(128)(4,1)}), s8[4194304]{0:T(1024)(128)(4,1)S(1)}, s32[]{:S(2)}) async-start(s8[8388608]{0:T(1024)(128)(4,1)} %bitcast.79), calls=%async_computation.1 | async-start | bytes 8388608

commit v2 on v1

--- a/solution.py
+++ b/solution.py
@@ -26,8 +26,12 @@
 class Ring:
     def __init__(self, n, items, sems):
         self.n, self.items = n, items
-        self.ring_send, self.ring_recv, self.side_send, self.side_recv, self.local = sems
+        self.ring_send, self.ring_recv, self.side_send, self.side_recv, self.local = sems[:5]
+        self.pair_sems = sems[5:]
         self.me = lax.axis_index("dp")
+        self.group = lax.axis_index("group")
+        self.half = lax.rem(self.group, 2)
+        self.pairs = {}
         self.lane = lax.axis_index("adapter")
         self.pos = ring_position(self.me, n)
         self.right = ring_device(self.pos + 1, n)
@@ -45,16 +49,21 @@
             return (0, rows // 2) if way == 0 else (rows // 2, rows // 2)
         return (0, rows) if way == 0 else (0, 0)
 
-    def target_rows(self, item, device, lane, start, count):
+    def target_rows(self, item, device, lane, start, count, half=None):
         rows = item[2]
-        return item[1].at[pl.ds(pl.multiple_of((device * 2 + lane) * rows + start, 16), count)]
+        if item[3]:
+            half = self.half if half is None else half
+            block = device * 4 + half * 2 + lane
+        else:
+            block = device * 2 + lane
+        return item[1].at[pl.ds(pl.multiple_of(block * rows + start, 16), count)]
 
     def begin(self):
         for i, item in enumerate(self.items):
             source, target, rows, shared = item
             if shared:
                 own = pltpu.make_async_copy(
-                    source, target.at[pl.ds(pl.multiple_of(self.me * 2 * rows, 16), 2 * rows)], self.local.at[i]
+                    source, target.at[pl.ds(pl.multiple_of(self.me * 4 * rows, 16), 4 * rows)], self.local.at[i]
                 )
             else:
                 own = pltpu.make_async_copy(
@@ -78,7 +87,9 @@
             device = ring_device(self.pos + back, self.n)
             target = self.target_rows(item, device, self.lane, start, count)
             if step == 0:
-                base = pl.multiple_of(self.lane * item[2] + start, 16) if item[3] else start
+                base = start
+                if item[3]:
+                    base = pl.multiple_of((self.half * 2 + self.lane) * item[2] + start, 16)
                 source = item[0].at[pl.ds(base, count)]
             else:
                 source = target
@@ -93,11 +104,23 @@
             copy.start()
             self.copies[i, way, step] = copy
 
-    def side(self, i, source, device, start, count, slot):
+    def pair(self, i, block, slot):
+        copy = pltpu.make_async_remote_copy(
+            src_ref=block,
+            dst_ref=block,
+            send_sem=self.pair_sems[0].at[i, slot],
+            recv_sem=self.pair_sems[1].at[i, slot],
+            device_id={"group": self.group + 1 - 2 * self.half},
+            device_id_type=MESH,
+        )
+        copy.start()
+        self.pairs[i, slot] = copy
+
+    def side(self, i, source, device, start, count, slot, half=None):
         item = self.items[i]
         copy = pltpu.make_async_remote_copy(
             src_ref=source,
-            dst_ref=self.target_rows(item, device, self.lane, start, count),
+            dst_ref=self.target_rows(item, device, self.lane, start, count, half),
             send_sem=self.side_send.at[i, slot],
             recv_sem=self.side_recv.at[i, slot],
             device_id={"adapter": 1 - self.lane},
@@ -105,6 +128,14 @@
         )
         copy.start()
         self.sides.append(copy)
+
+    def arrived(self, step):
+        for i, item in enumerate(self.items):
+            for way in (0, 1):
+                start, count = self.window(item, None, step, way)
+                if count:
+                    ahead = self.n - 1 - step if way == 0 else 1 + step
+                    yield i, 1 + 2 * step + way, ring_device(self.pos + ahead, self.n), start, count
 
     def run(self):
         for step in range(self.steps):
@@ -114,17 +145,28 @@
                         self.copies[i, way, step].wait_recv()
                 if step + 1 < self.steps:
                     self.send(i, step + 1)
-                for way in (0, 1):
-                    start, count = self.window(item, None, step, way)
-                    if count == 0:
-                        continue
-                    ahead = self.n - 1 - step if way == 0 else 1 + step
-                    device = ring_device(self.pos + ahead, self.n)
-                    block = self.target_rows(item, device, self.lane, start, count)
-                    self.side(i, block, device, start, count, 1 + 2 * step + way)
+            for i, slot, device, start, count in self.arrived(step):
+                item = self.items[i]
+                block = self.target_rows(item, device, self.lane, start, count)
+                if item[3]:
+                    self.pair(i, block, slot)
+                self.side(i, block, device, start, count, slot)
+            if step:
+                self.cross(step - 1)
+        self.cross(self.steps - 1)
+
+    def cross(self, step):
+        for i, slot, device, start, count in self.arrived(step):
+            item = self.items[i]
+            if item[3]:
+                self.pairs[i, slot].wait_recv()
+                block = self.target_rows(item, device, self.lane, start, count, 1 - self.half)
+                self.side(i, block, device, start, count, self.n + slot, 1 - self.half)
 
     def finish(self):
         for copy in self.copies.values():
+            copy.wait_send()
+        for copy in self.pairs.values():
             copy.wait_send()
         for copy in self.sides:
             copy.wait()
@@ -136,10 +178,10 @@
     return [
         pltpu.SemaphoreType.DMA((items, 2, n // 2)),
         pltpu.SemaphoreType.DMA((items, 2, n // 2)),
-        pltpu.SemaphoreType.DMA((items, 1 + n)),
-        pltpu.SemaphoreType.DMA((items, 1 + n)),
+        pltpu.SemaphoreType.DMA((items, 1 + 2 * n)),
+        pltpu.SemaphoreType.DMA((items, 1 + 2 * n)),
         pltpu.SemaphoreType.DMA((items,)),
-    ]
+    ] + [pltpu.SemaphoreType.DMA((items, 1 + n))] * 2
 
 
 def greet_ring(barrier, n):
@@ -160,7 +202,7 @@
 
 def weight_kernel(n, weight_ref, down_ref, up_ref, hot_ref, weight_out, down_out, up_out, hot_out, *sems):
     devices = 2 * n
-    ring_sems, (send_sem, recv_sem, local_sem) = sems[:5], sems[5:]
+    ring_sems, (send_sem, recv_sem, local_sem) = sems[:7], sems[7:]
     me = lax.axis_index("dp") * 2 + lax.axis_index("adapter")
     barrier = pltpu.get_barrier_semaphore()
 
@@ -173,7 +215,10 @@
         return carry
 
     lax.fori_loop(1, devices, greet, 0)
-    pl.semaphore_wait(barrier, devices - 1)
+    group = lax.axis_index("group")
+    other = group + 1 - 2 * lax.rem(group, 2)
+    pl.semaphore_signal(barrier, inc=1, device_id={"group": other}, device_id_type=MESH)
+    pl.semaphore_wait(barrier, devices)
 
     rows_down, rows_up = down_out.shape[0], up_out.shape[0]
     wide = down_ref.shape[1]
@@ -200,7 +245,7 @@
             for i, (source, target) in enumerate(parts(peer, me))
         ]
 
-    ring = Ring(n, [(weight_ref, weight_out, weight_ref.shape[0] // 2, True)], ring_sems)
+    ring = Ring(n, [(weight_ref, weight_out, weight_ref.shape[0] // 4, True)], ring_sems)
 
     def start(k, carry):
         for copy in copies(k):
@@ -237,6 +282,35 @@
         scratch_shapes=scratch,
         compiler_params=pltpu.CompilerParams(collective_id=collective_id, has_side_effects=True),
     )(*operands)
+
+
+def input_gradient_kernel(grad_ref, weight_ref, lora_ref, down_ref, out_ref):
+    total = dot(grad_ref[...], weight_ref[...], 1, 1) + dot(lora_ref[...], down_ref[...], 1, 1)
+    out_ref[...] = total.astype(out_ref.dtype)
+
+
+def input_gradients(output_gradient, weight, lora_grad, down):
+    tok, outputs = output_gradient.shape
+    width, flat = down.shape
+    columns = 512
+    return pl.pallas_call(
+        input_gradient_kernel,
+        grid=(width // columns,),
+        out_shape=jax.ShapeDtypeStruct((tok, width), output_gradient.dtype),
+        in_specs=[
+            pl.BlockSpec((tok, outputs), lambda i: (0, 0)),
+            pl.BlockSpec((columns, outputs), lambda i: (i, 0)),
+            pl.BlockSpec((tok, flat), lambda i: (0, 0)),
+            pl.BlockSpec((columns, flat), lambda i: (i, 0)),
+        ],
+        out_specs=pl.BlockSpec((tok, columns), lambda i: (0, i)),
+        compiler_params=pltpu.CompilerParams(vmem_limit_bytes=32 * 1024 * 1024),
+        cost_estimate=pl.CostEstimate(
+            flops=2 * tok * width * (outputs + flat),
+            bytes_accessed=2 * (width * (outputs + flat) + tok * (outputs + flat + width)),
+            transcendentals=0,
+        ),
+    )(output_gradient, weight, lora_grad, down)
 
 
 def token_slots(segment_length_quota, segment_tenant_id, tenant_adapter_slot, tok):
@@ -325,7 +399,7 @@
     down_map_gradient = dot(spread, down_parts, 0, 1).reshape(slots, rank, down_columns)
     up_map_gradient = dot(spread, up_parts, 0, 1).reshape(slots, rank, up_columns)
 
-    input_gradient = (dot(output_gradient, weight, 1, 1) + dot(lora_grad, down, 1, 1)).astype(bf16)
+    input_gradient = input_gradients(output_gradient, weight, lora_grad, down)
     return (input_gradient, down_map_gradient, up_map_gradient)
 
 

time: 158 us -> 156 us (0.987)
  Pallas kernels: 112 us -> 121 us
  matrix products: 28.3 us -> 20.3 us
    pallas_call x0 -> x1, Pallas kernels: none -> 8.93 us  [input_gradients(): pl.pallas_call(input_gradient_kernel, grid=(width // columns,), out_shape...]
    dot_general x9 -> x7, matrix products: 28.3 us -> 20.3 us  [dot(): lax.dot_general(left, right, (((left_dim,), (right_dim,)), ((), ())), pre...]
    unnamed x11 -> x8, local copies, waits for them, and re-layouts: 6.36 us -> 2.2 us
where the time goes in v2:
time: 156 us; the launch traced here: 155 us
  Pallas kernels  121 us (78%)
  matrix products  20.3 us (13%)
  local copies, waits for them, and re-layouts  9.44 us (6%)
  other arithmetic  3.81 us (2%)
    pallas_call x2, Pallas kernels, call(): pl.pallas_call(kernel, out_shape=outs, in_specs=[anywhere] * len(operands...  112 us
    dot_general x7, matrix products, dot(): lax.dot_general(left, right, (((left_dim,), (right_dim,)), ((), ())), pre...  20.3 us
    pallas_call x1, Pallas kernels, input_gradients(): pl.pallas_call(input_gradient_kernel, grid=(width // columns,), out_shape...  8.93 us

profile of v2, /device:TPU:13, one launch (start us, length us, event | category | flops | bytes accessed | tf_op | source)
XLA Modules:
  0.0 154.9 jit_solution(756072293509910826)
XLA Ops:
  0.6 0.0 copy-start
  0.6 0.9 reduce-window.4
  1.6 0.7 fusion.29
  2.2 0.9 select_reduce_fusion
  3.1 0.3 fusion.25
  3.3 1.1 broadcast_in_dim.10
  4.4 1.6 %copy.28 = f32[512,512]{1,0:T(8,128)S(1)} copy(f32[512,512]{0,1:T(8,128)} %bitcast.61) | data formatting | bytes 2097152 | tf_op jit(solution)/shard_map/reshape | solution.py:366
  6.0 1.8 %copy.25 = bf16[512,256]{0,1:T(8,128)(2,1)} copy(bf16[512,256]{1,0:T(8,128)(2,1)} %bitcast.67) | data formatting | bytes 524288 | tf_op jit(solution)/shard_map/reshape | solution.py:352
  7.8 1.6 %copy.26 = bf16[512,64]{0,1:T(8,128)(2,1)} copy(bf16[512,64]{1,0:T(8,128)(2,1)} %bitcast.68) | data formatting | bytes 131072 | tf_op jit(solution)/shard_map/reshape | solution.py:353
  9.4 32.2 %shard_map.103 = (bf16[4096,512]{1,0:T(8,128)(2,1)}, bf16[1024,512]{1,0:T(8,128)(2,1)}) custom-call(bf16[256,512]{1,0:T(8,128)(2,1)} %bitcast.64, bf16[64,512]{1,0:T(8,128)(2,1)} %bitcast.66), custom_call_target="tpu_custom_call" | custom-call | tf_op jit(solution)/shard_map/pallas_call | solution.py:277
  41.7 0.0 copy-done
  41.7 1.9 %fusion.5.lora_ref = bf16[512,512]{1,0:T(8,128)(2,1)S(1)} fusion(f32[512,512]{1,0:T(8,128)S(1)} %copy.28, bf16[512,1024]{1,0:T(8,128)(2,1)S(1)} %copy-done, bf16[1024,512]{1,0:T(8,128)(2,1)} %get-tuple-element.9), kind=kOutput, calls=%fused_computation.9 | convolution fusion | flops 537657344 | bytes 3670016 | tf_op jit(solution)/shard_map/dot_general | solution.py:328
  43.6 0.0 copy-start.3
  43.6 0.1 fusion.24
  43.7 0.1 copy.29
  43.9 5.2 %fusion.down_ref = bf16[4096,128]{1,0:T(8,128)(2,1)} fusion(bf16[512,4096]{1,0:T(8,128)(2,1)} %param.8, f32[512,128]{1,0:T(8,128)S(1)} %copy.29, bf16[512,512]{1,0:T(8,128)(2,1)S(1)} %fusion.5.lora_ref, s32[128]{0:T(128)S(1)} %iota_and_fusion.2, s32[512]{0:T(512)S(1)} %iota_and_fusion.1), kind=kOutput, calls=%fused_computation.1 | convolution fusion | flops 604700672 | bytes 6031872 | tf_op jit(solution)/shard_map/dot_general | solution.py:328
  49.0 0.0 copy-done.3
  49.0 6.3 %fusion.9 = bf16[512,128]{1,0:T(8,128)(2,1)S(1)} fusion(f32[512,128]{1,0:T(8,128)S(1)} %copy.29, f32[512,512]{0,1:T(8,128)S(1)} %bitcast.62, bf16[4096,512]{1,0:T(8,128)(2,1)} %get-tuple-element.10.down_ref, bf16[512,4096]{1,0:T(8,128)(2,1)} %param.8, s32[128]{0:T(128)S(1)} %iota_and_fusion.2, s32[512]{0:T(512)S(1)} %iota_and_fusion.1), kind=kOutput, calls=%fused_computation.16 | convolution fusion | flops 2215313408 | bytes 9832960 | tf_op jit(solution)/shard_map/dot_general | solution.py:328
  55.3 1.3 fusion.7.up_ref
  56.6 0.1 iota_compare_fusion.2
  56.6 0.6 pad_convert_fusion.hot_ref
  57.2 79.5 %shard_map.104 = (bf16[4096,1024]{1,0:T(8,128)(2,1)}, bf16[256,2048]{1,0:T(8,128)(2,1)}, bf16[64,2048]{1,0:T(8,128)(2,1)}, bf16[16,16,128]{2,1,0:T(8,128)(2,1)}) custom-call(bf16[512,1024]{1,0:T(8,128)(2,1)} %weight_ref.1, bf16[4096,128]{1,0:T(8,128)(2,1)} %fusion.down_ref, bf16[1024,128]{1,0:T(8,128)(2,1)} %fusion.7.up_ref, ...), custom_call_target="tpu_custom_call" | custom-call | tf_op jit(solution)/shard_map/pallas_call | solution.py:277
  136.7 0.8 slice_bitcast_fusion
  137.5 0.1 broadcast_in_dim.12
  137.6 0.2 copy.33
  137.8 0.0 copy-start.1
  137.8 0.6 compare_select_fusion
  138.4 2.6 %fusion.15 = f32[32,16,64]{2,1,0:T(8,128)} fusion(bf16[32,16,2048]{2,1,0:T(8,128)(2,1)S(1)} %bitcast.59, bf16[64,2048]{1,0:T(8,128)(2,1)} %get-tuple-element.14), kind=kOutput, calls=%fused_computation.21 | convolution fusion | flops 134217728 | bytes 2490368 | tf_op jit(solution)/shard_map/dot_general | solution.py:328
  141.0 2.8 %fusion.10 = f32[32,16,256]{2,1,0:T(8,128)} fusion(bf16[32,16,2048]{2,1,0:T(8,128)(2,1)S(1)} %bitcast.60, bf16[256,2048]{1,0:T(8,128)(2,1)} %get-tuple-element.13), kind=kOutput, calls=%fused_computation.17 | convolution fusion | flops 536870912 | bytes 3670016 | tf_op jit(solution)/shard_map/dot_general | solution.py:328
  143.8 0.0 copy-done.1
  143.8 0.0 copy-start.2
  143.8 2.2 %copy-done.2 = bf16[4096,512]{1,0:T(8,128)(2,1)S(1)} copy-done((bf16[4096,512]{1,0:T(8,128)(2,1)S(1)}, bf16[4096,512]{1,0:T(8,128)(2,1)}, u32[]{:S(2)}) %copy-start.2) | copy-done | bytes 4194328
  146.0 8.9 %shard_map.105 = bf16[512,4096]{1,0:T(8,128)(2,1)} custom-call(bf16[512,1024]{1,0:T(8,128)(2,1)S(1)} %copy-done, bf16[4096,1024]{1,0:T(8,128)(2,1)S(1)} %copy-done.1, bf16[512,512]{1,0:T(8,128)(2,1)S(1)} %fusion.5.lora_ref, bf16[4096,512]{1,0:T(8,128)(2,1)S(1)} %copy-done.2), custom_call_target="tpu_custom_call" | custom-call | flops 6442450944 | bytes 18350080 | tf_op jit(solution)/shard_map/pallas_call | solution.py:296
  (4 shorter events, 0.0 us)
Async XLA Ops:
  0.6 41.0 %copy-start = (bf16[512,1024]{1,0:T(8,128)(2,1)S(1)}, bf16[512,1024]{1,0:T(8,128)(2,1)}, u32[]{:S(2)}) copy-start(bf16[512,1024]{1,0:T(8,128)(2,1)} %grad_ref.1) | copy-start | bytes 3145732
  43.6 5.4 %copy-start.3 = (f32[512,32,16]{0,2,1:T(8,128)S(1)}, f32[512,32,16]{0,2,1:T(8,128)}, u32[]{:S(2)}) copy-start(f32[512,32,16]{0,2,1:T(8,128)} %broadcast_in_dim.10) | copy-start | bytes 3145732
  137.8 6.0 %copy-start.1 = (bf16[4096,1024]{1,0:T(8,128)(2,1)S(1)}, bf16[4096,1024]{1,0:T(8,128)(2,1)}, u32[]{:S(2)}) copy-start(bf16[4096,1024]{1,0:T(8,128)(2,1)} %get-tuple-element.11.weight_ref) | copy-start | bytes 25165828
  143.8 2.2 %copy-start.2 = (bf16[4096,512]{1,0:T(8,128)(2,1)S(1)}, bf16[4096,512]{1,0:T(8,128)(2,1)}, u32[]{:S(2)}) copy-start(bf16[4096,512]{1,0:T(8,128)(2,1)} %get-tuple-element.10.down_ref) | copy-start | bytes 12582916

commit v3 on v2

--- a/solution.py
+++ b/solution.py
@@ -59,23 +59,22 @@
         return item[1].at[pl.ds(pl.multiple_of(block * rows + start, 16), count)]
 
     def begin(self):
-        for i, item in enumerate(self.items):
-            source, target, rows, shared = item
-            if shared:
-                own = pltpu.make_async_copy(
-                    source, target.at[pl.ds(pl.multiple_of(self.me * 4 * rows, 16), 4 * rows)], self.local.at[i]
-                )
-            else:
-                own = pltpu.make_async_copy(
-                    source, self.target_rows(item, self.me, self.lane, 0, rows), self.local.at[i]
-                )
-            own.start()
-            self.locals.append(own)
         for i in range(len(self.items)):
             self.send(i, 0)
         for i, item in enumerate(self.items):
             if not item[3]:
                 self.side(i, item[0], self.me, 0, item[2], 0)
+        for i, (source, target, rows, shared) in enumerate(self.items):
+            cuts = 4 if shared else 1
+            for cut in range(cuts):
+                block = self.me * 4 + cut if shared else self.me * 2 + self.lane
+                own = pltpu.make_async_copy(
+                    source.at[pl.ds(cut * rows, rows)],
+                    target.at[pl.ds(pl.multiple_of(block * rows, 16), rows)],
+                    self.local.at[i, cut],
+                )
+                own.start()
+                self.locals.append(own)
 
     def send(self, i, step):
         item = self.items[i]
@@ -180,7 +179,7 @@
         pltpu.SemaphoreType.DMA((items, 2, n // 2)),
         pltpu.SemaphoreType.DMA((items, 1 + 2 * n)),
         pltpu.SemaphoreType.DMA((items, 1 + 2 * n)),
-        pltpu.SemaphoreType.DMA((items,)),
+        pltpu.SemaphoreType.DMA((items, 4)),
     ] + [pltpu.SemaphoreType.DMA((items, 1 + n))] * 2
 
 
@@ -189,20 +188,27 @@
     for device in (ring_device(pos + 1, n), ring_device(pos + n - 1, n)):
         pl.semaphore_signal(barrier, inc=1, device_id={"dp": device}, device_id_type=MESH)
     pl.semaphore_signal(barrier, inc=1, device_id={"adapter": 1 - lane}, device_id_type=MESH)
-    pl.semaphore_wait(barrier, 3)
-
-
-def maps_kernel(n, down_ref, up_ref, down_out, up_out, *sems):
+    group = lax.axis_index("group")
+    other = group + 1 - 2 * lax.rem(group, 2)
+    pl.semaphore_signal(barrier, inc=1, device_id={"group": other}, device_id_type=MESH)
+    pl.semaphore_wait(barrier, 4)
+
+
+def gather_kernel(n, weight_ref, down_ref, up_ref, weight_out, down_out, up_out, *sems):
     greet_ring(pltpu.get_barrier_semaphore(), n)
-    ring = Ring(n, [(down_ref, down_out, down_ref.shape[0], False), (up_ref, up_out, up_ref.shape[0], False)], sems)
+    items = [
+        (weight_ref, weight_out, weight_ref.shape[0] // 4, True),
+        (down_ref, down_out, down_ref.shape[0], False),
+        (up_ref, up_out, up_ref.shape[0], False),
+    ]
+    ring = Ring(n, items, sems)
     ring.begin()
     ring.run()
     ring.finish()
 
 
-def weight_kernel(n, weight_ref, down_ref, up_ref, hot_ref, weight_out, down_out, up_out, hot_out, *sems):
+def exchange_kernel(n, down_ref, up_ref, hot_ref, down_out, up_out, hot_out, send_sem, recv_sem, local_sem):
     devices = 2 * n
-    ring_sems, (send_sem, recv_sem, local_sem) = sems[:7], sems[7:]
     me = lax.axis_index("dp") * 2 + lax.axis_index("adapter")
     barrier = pltpu.get_barrier_semaphore()
 
@@ -215,10 +221,7 @@
         return carry
 
     lax.fori_loop(1, devices, greet, 0)
-    group = lax.axis_index("group")
-    other = group + 1 - 2 * lax.rem(group, 2)
-    pl.semaphore_signal(barrier, inc=1, device_id={"group": other}, device_id_type=MESH)
-    pl.semaphore_wait(barrier, devices)
+    pl.semaphore_wait(barrier, devices - 1)
 
     rows_down, rows_up = down_out.shape[0], up_out.shape[0]
     wide = down_ref.shape[1]
@@ -245,8 +248,6 @@
             for i, (source, target) in enumerate(parts(peer, me))
         ]
 
-    ring = Ring(n, [(weight_ref, weight_out, weight_ref.shape[0] // 4, True)], ring_sems)
-
     def start(k, carry):
         for copy in copies(k):
             copy.start()
@@ -255,12 +256,9 @@
     own = [
         pltpu.make_async_copy(source, target, local_sem.at[i]) for i, (source, target) in enumerate(parts(me, me))
     ]
+    lax.fori_loop(1, devices, start, 0)
     for copy in own:
         copy.start()
-    ring.begin()
-    lax.fori_loop(1, devices, start, 0)
-    ring.run()
-    ring.finish()
 
     def end(k, carry):
         for copy in copies(k):
@@ -351,11 +349,15 @@
 
     down_own = adapter_down_maps.reshape(flat, down_columns).T
     up_own = adapter_up_maps.reshape(flat, up_columns).T
-    down, up = call(
-        functools.partial(maps_kernel, n),
-        [jax.ShapeDtypeStruct((width, flat), bf16), jax.ShapeDtypeStruct((outputs, flat), bf16)],
-        [down_own, up_own],
-        ring_scratch(n, 2),
+    weight, down, up = call(
+        functools.partial(gather_kernel, n),
+        [
+            jax.ShapeDtypeStruct((width, outputs), bf16),
+            jax.ShapeDtypeStruct((width, flat), bf16),
+            jax.ShapeDtypeStruct((outputs, flat), bf16),
+        ],
+        [frozen_value_weight, down_own, up_own],
+        ring_scratch(n, 3),
         0,
     )
 
@@ -376,17 +378,15 @@
     up_term = (adapter_scale * dot(output_gradient, lora_in_seg, 0, 0)).astype(bf16)
 
     hot = jnp.pad(slot_hot.astype(bf16), ((0, 16 - segs % 16), (0, 128 - slots % 128)))
-    weight, down_parts, up_parts, hots = call(
-        functools.partial(weight_kernel, n),
+    down_parts, up_parts, hots = call(
+        functools.partial(exchange_kernel, n),
         [
-            jax.ShapeDtypeStruct((width, outputs), bf16),
             jax.ShapeDtypeStruct((down_columns, devices * wide), bf16),
             jax.ShapeDtypeStruct((up_columns, devices * wide), bf16),
             jax.ShapeDtypeStruct((devices,) + hot.shape, bf16),
         ],
-        [frozen_value_weight, down_term, up_term, hot],
-        ring_scratch(n, 1)
-        + [pltpu.SemaphoreType.DMA((3, devices)), pltpu.SemaphoreType.DMA((3, devices)), pltpu.SemaphoreType.DMA((3,))],
+        [down_term, up_term, hot],
+        [pltpu.SemaphoreType.DMA((3, devices)), pltpu.SemaphoreType.DMA((3, devices)), pltpu.SemaphoreType.DMA((3,))],
         1,
     )
 

time: 156 us -> 142 us (0.910)
  Pallas kernels: 121 us -> 107 us
    pallas_call x2, Pallas kernels: 112 us -> 98.3 us  [call(): pl.pallas_call(kernel, out_shape=outs, in_specs=[anywhere] * len(operands...]
    unnamed x8, local copies, waits for them, and re-layouts: 2.2 us -> 5.57 us
where the time goes in v3:
time: 142 us; the launch traced here: 141 us
  Pallas kernels  107 us (75%)
  matrix products  19 us (13%)
  local copies, waits for them, and re-layouts  10.6 us (7%)
  other arithmetic  3.72 us (3%)
    pallas_call x2, Pallas kernels, call(): pl.pallas_call(kernel, out_shape=outs, in_specs=[anywhere] * len(operands...  98.3 us
    dot_general x7, matrix products, dot(): lax.dot_general(left, right, (((left_dim,), (right_dim,)), ((), ())), pre...  19 us
    pallas_call x1, Pallas kernels, input_gradients(): pl.pallas_call(input_gradient_kernel, grid=(width // columns,), out_shape...  8.93 us
    unnamed x8, local copies, waits for them, and re-layouts  5.57 us

profile of v3, /device:TPU:13, one launch (start us, length us, event | category | flops | bytes accessed | tf_op | source)
XLA Modules:
  0.0 141.4 jit_solution(4757536516779974316)
XLA Ops:
  0.6 0.9 select_reduce_fusion
  1.5 0.8 reduce-window.4
  2.3 0.7 fusion.29
  3.0 0.1 iota_compare_fusion.2
  3.1 0.6 pad_convert_fusion.hot_ref
  3.7 0.1 fusion.24
  3.7 0.3 fusion.25
  4.0 1.6 %copy.26 = bf16[512,64]{0,1:T(8,128)(2,1)} copy(bf16[512,64]{1,0:T(8,128)(2,1)} %bitcast.68) | data formatting | bytes 131072 | tf_op jit(solution)/shard_map/reshape | solution.py:351
  5.6 0.1 copy.29
  5.8 1.8 %copy.25 = bf16[512,256]{0,1:T(8,128)(2,1)} copy(bf16[512,256]{1,0:T(8,128)(2,1)} %bitcast.66) | data formatting | bytes 524288 | tf_op jit(solution)/shard_map/reshape | solution.py:350
  7.6 0.1 broadcast_in_dim.10
  7.7 0.3 copy.28
  8.0 64.1 %shard_map.103 = (bf16[4096,1024]{1,0:T(8,128)(2,1)}, bf16[4096,512]{1,0:T(8,128)(2,1)}, bf16[1024,512]{1,0:T(8,128)(2,1)}) custom-call(bf16[512,1024]{1,0:T(8,128)(2,1)} %weight_ref.1, bf16[256,512]{1,0:T(8,128)(2,1)} %bitcast.65, bf16[64,512]{1,0:T(8,128)(2,1)} %bitcast.67), custom_call_target="tpu_custom_call" | custom-call | tf_op jit(solution)/shard_map/pallas_call | solution.py:275
  72.2 0.0 copy-start
  72.2 6.3 %fusion.9 = bf16[512,128]{1,0:T(8,128)(2,1)S(1)} fusion(f32[512,128]{1,0:T(8,128)S(1)} %copy.29, f32[512,512]{0,1:T(8,128)S(1)} %bitcast.62, bf16[4096,512]{1,0:T(8,128)(2,1)} %get-tuple-element.11.down_ref, bf16[512,4096]{1,0:T(8,128)(2,1)} %param.8, s32[128]{0:T(128)S(1)} %iota_and_fusion.2, s32[512]{0:T(512)S(1)} %iota_and_fusion.1), kind=kOutput, calls=%fused_computation.16 | convolution fusion | flops 2215313408 | bytes 9832960 | tf_op jit(solution)/shard_map/dot_general | solution.py:326
  78.5 0.0 copy-done
  78.5 1.9 %fusion.5.lora_ref = bf16[512,512]{1,0:T(8,128)(2,1)S(1)} fusion(f32[512,512]{1,0:T(8,128)S(1)} %copy.28, bf16[512,1024]{1,0:T(8,128)(2,1)S(1)} %copy-done, bf16[1024,512]{1,0:T(8,128)(2,1)} %get-tuple-element.10), kind=kOutput, calls=%fused_computation.9 | convolution fusion | flops 537657344 | bytes 3670016 | tf_op jit(solution)/shard_map/dot_general | solution.py:326
  80.4 0.0 copy-start.1
  80.5 3.4 %copy-done.1 = bf16[4096,1024]{1,0:T(8,128)(2,1)S(1)} copy-done((bf16[4096,1024]{1,0:T(8,128)(2,1)S(1)}, bf16[4096,1024]{1,0:T(8,128)(2,1)}, u32[]{:S(2)}) %copy-start.1) | copy-done | bytes 8388632
  83.8 0.0 copy-start.2
  83.8 2.2 %copy-done.2 = bf16[4096,512]{1,0:T(8,128)(2,1)S(1)} copy-done((bf16[4096,512]{1,0:T(8,128)(2,1)S(1)}, bf16[4096,512]{1,0:T(8,128)(2,1)}, u32[]{:S(2)}) %copy-start.2) | copy-done | bytes 4194328
  86.0 8.9 %shard_map.104 = bf16[512,4096]{1,0:T(8,128)(2,1)} custom-call(bf16[512,1024]{1,0:T(8,128)(2,1)S(1)} %copy-done, bf16[4096,1024]{1,0:T(8,128)(2,1)S(1)} %copy-done.1, bf16[512,512]{1,0:T(8,128)(2,1)S(1)} %fusion.5.lora_ref, bf16[4096,512]{1,0:T(8,128)(2,1)S(1)} %copy-done.2), custom_call_target="tpu_custom_call" | custom-call | flops 6442450944 | bytes 18350080 | tf_op jit(solution)/shard_map/pallas_call | solution.py:294
  95.0 1.3 fusion.7.up_ref
  96.2 5.1 %fusion.down_ref = bf16[4096,128]{1,0:T(8,128)(2,1)} fusion(bf16[512,4096]{1,0:T(8,128)(2,1)} %param.8, f32[512,128]{1,0:T(8,128)S(1)} %copy.29, bf16[512,512]{1,0:T(8,128)(2,1)S(1)} %fusion.5.lora_ref, s32[128]{0:T(128)S(1)} %iota_and_fusion.2, s32[512]{0:T(512)S(1)} %iota_and_fusion.1), kind=kOutput, calls=%fused_computation.1 | convolution fusion | flops 604700672 | bytes 6031872 | tf_op jit(solution)/shard_map/dot_general | solution.py:326
  101.3 34.2 %shard_map.105 = (bf16[256,2048]{1,0:T(8,128)(2,1)}, bf16[64,2048]{1,0:T(8,128)(2,1)}, bf16[16,16,128]{2,1,0:T(8,128)(2,1)}) custom-call(bf16[4096,128]{1,0:T(8,128)(2,1)} %fusion.down_ref, bf16[1024,128]{1,0:T(8,128)(2,1)} %fusion.7.up_ref, bf16[16,128]{1,0:T(8,128)(2,1)} %pad_convert_fusion.hot_ref), custom_call_target="tpu_custom_call" | custom-call | tf_op jit(solution)/shard_map/pallas_call | solution.py:275
  135.5 0.0 copy-start.3
  135.5 0.8 slice_bitcast_fusion
  136.3 0.1 broadcast_in_dim.12
  136.4 0.2 copy.33
  136.6 0.6 compare_select_fusion
  137.2 2.8 %fusion.10 = f32[32,16,256]{2,1,0:T(8,128)} fusion(bf16[32,16,2048]{2,1,0:T(8,128)(2,1)S(1)} %bitcast.59, bf16[256,2048]{1,0:T(8,128)(2,1)} %get-tuple-element.13), kind=kOutput, calls=%fused_computation.17 | convolution fusion | flops 536870912 | bytes 3670016 | tf_op jit(solution)/shard_map/dot_general | solution.py:326
  140.0 0.0 copy-done.3
  140.0 1.4 fusion.15
  (4 shorter events, 0.0 us)
Async XLA Ops:
  72.2 6.3 %copy-start = (bf16[512,1024]{1,0:T(8,128)(2,1)S(1)}, bf16[512,1024]{1,0:T(8,128)(2,1)}, u32[]{:S(2)}) copy-start(bf16[512,1024]{1,0:T(8,128)(2,1)} %grad_ref.1) | copy-start | bytes 3145732
  80.4 3.4 %copy-start.1 = (bf16[4096,1024]{1,0:T(8,128)(2,1)S(1)}, bf16[4096,1024]{1,0:T(8,128)(2,1)}, u32[]{:S(2)}) copy-start(bf16[4096,1024]{1,0:T(8,128)(2,1)} %get-tuple-element.9.weight_ref) | copy-start | bytes 25165828
  83.8 2.2 %copy-start.2 = (bf16[4096,512]{1,0:T(8,128)(2,1)S(1)}, bf16[4096,512]{1,0:T(8,128)(2,1)}, u32[]{:S(2)}) copy-start(bf16[4096,512]{1,0:T(8,128)(2,1)} %get-tuple-element.11.down_ref) | copy-start | bytes 12582916
  135.5 4.5 %copy-start.3 = (bf16[64,2048]{1,0:T(8,128)(2,1)S(1)}, bf16[64,2048]{1,0:T(8,128)(2,1)}, u32[]{:S(2)}) copy-start(bf16[64,2048]{1,0:T(8,128)(2,1)} %get-tuple-element.14) | copy-start | bytes 786436

commit v4 on v3

--- a/solution.py
+++ b/solution.py
@@ -207,7 +207,8 @@
     ring.finish()
 
 
-def exchange_kernel(n, down_ref, up_ref, hot_ref, down_out, up_out, hot_out, send_sem, recv_sem, local_sem):
+def exchange_kernel(n, down_ref, up_ref, hot_ref, grad_ref, weight_ref, lora_ref, maps_ref, *rest):
+    down_out, up_out, hot_out, input_out, send_sem, recv_sem, local_sem = rest
     devices = 2 * n
     me = lax.axis_index("dp") * 2 + lax.axis_index("adapter")
     barrier = pltpu.get_barrier_semaphore()
@@ -259,6 +260,7 @@
     lax.fori_loop(1, devices, start, 0)
     for copy in own:
         copy.start()
+    input_gradient_pipeline((grad_ref, weight_ref, lora_ref, maps_ref), input_out)
 
     def end(k, carry):
         for copy in copies(k):
@@ -278,7 +280,9 @@
         in_specs=[anywhere] * len(operands),
         out_specs=[anywhere] * len(outs),
         scratch_shapes=scratch,
-        compiler_params=pltpu.CompilerParams(collective_id=collective_id, has_side_effects=True),
+        compiler_params=pltpu.CompilerParams(
+            collective_id=collective_id, has_side_effects=True, vmem_limit_bytes=32 * 1024 * 1024
+        ),
     )(*operands)
 
 
@@ -287,28 +291,22 @@
     out_ref[...] = total.astype(out_ref.dtype)
 
 
-def input_gradients(output_gradient, weight, lora_grad, down):
+def input_gradient_pipeline(operands, out):
+    output_gradient, weight, lora_grad, down = operands
     tok, outputs = output_gradient.shape
     width, flat = down.shape
     columns = 512
-    return pl.pallas_call(
+    pltpu.emit_pipeline(
         input_gradient_kernel,
         grid=(width // columns,),
-        out_shape=jax.ShapeDtypeStruct((tok, width), output_gradient.dtype),
         in_specs=[
             pl.BlockSpec((tok, outputs), lambda i: (0, 0)),
             pl.BlockSpec((columns, outputs), lambda i: (i, 0)),
             pl.BlockSpec((tok, flat), lambda i: (0, 0)),
             pl.BlockSpec((columns, flat), lambda i: (i, 0)),
         ],
-        out_specs=pl.BlockSpec((tok, columns), lambda i: (0, i)),
-        compiler_params=pltpu.CompilerParams(vmem_limit_bytes=32 * 1024 * 1024),
-        cost_estimate=pl.CostEstimate(
-            flops=2 * tok * width * (outputs + flat),
-            bytes_accessed=2 * (width * (outputs + flat) + tok * (outputs + flat + width)),
-            transcendentals=0,
-        ),
-    )(output_gradient, weight, lora_grad, down)
+        out_specs=[pl.BlockSpec((tok, columns), lambda i: (0, i))],
+    )(output_gradient, weight, lora_grad, down, out)
 
 
 def token_slots(segment_length_quota, segment_tenant_id, tenant_adapter_slot, tok):
@@ -378,14 +376,15 @@
     up_term = (adapter_scale * dot(output_gradient, lora_in_seg, 0, 0)).astype(bf16)
 
     hot = jnp.pad(slot_hot.astype(bf16), ((0, 16 - segs % 16), (0, 128 - slots % 128)))
-    down_parts, up_parts, hots = call(
+    down_parts, up_parts, hots, input_gradient = call(
         functools.partial(exchange_kernel, n),
         [
             jax.ShapeDtypeStruct((down_columns, devices * wide), bf16),
             jax.ShapeDtypeStruct((up_columns, devices * wide), bf16),
             jax.ShapeDtypeStruct((devices,) + hot.shape, bf16),
+            jax.ShapeDtypeStruct((tok, width), bf16),
         ],
-        [down_term, up_term, hot],
+        [down_term, up_term, hot, output_gradient, weight, lora_grad, down],
         [pltpu.SemaphoreType.DMA((3, devices)), pltpu.SemaphoreType.DMA((3, devices)), pltpu.SemaphoreType.DMA((3,))],
         1,
     )
@@ -399,7 +398,6 @@
     down_map_gradient = dot(spread, down_parts, 0, 1).reshape(slots, rank, down_columns)
     up_map_gradient = dot(spread, up_parts, 0, 1).reshape(slots, rank, up_columns)
 
-    input_gradient = input_gradients(output_gradient, weight, lora_grad, down)
     return (input_gradient, down_map_gradient, up_map_gradient)
 
 

time: 142 us -> 137 us (0.965)
  local copies, waits for them, and re-layouts: 10.6 us -> 21 us
  Pallas kernels: 107 us -> 97 us
  matrix products: 19 us -> 15 us
    unnamed x8 -> x21, local copies, waits for them, and re-layouts: 5.57 us -> 15.8 us
    pallas_call x1 -> x0, Pallas kernels: 8.93 us -> none  [input_gradients(): pl.pallas_call(input_gradient_kernel, grid=(width // columns,), out_shape...]
    dot_general x7, matrix products: 19 us -> 15 us  [dot(): lax.dot_general(left, right, (((left_dim,), (right_dim,)), ((), ())), pre...]
where the time goes in v4:
time: 137 us
  Pallas kernels  97 us (71%)
  local copies, waits for them, and re-layouts  21 us (15%)
  matrix products  15 us (11%)
  other arithmetic  3.28 us (2%)
    pallas_call x2, Pallas kernels, call(): pl.pallas_call(kernel, out_shape=outs, in_specs=[anywhere] * len(operands...  97 us
    unnamed x21, local copies, waits for them, and re-layouts  15.8 us
    dot_general x7, matrix products, dot(): lax.dot_general(left, right, (((left_dim,), (right_dim,)), ((), ())), pre...  15 us

profile of v4, /device:TPU:13, one launch (start us, length us, event | category | flops | bytes accessed | tf_op | source)
XLA Modules:
  0.0 137.1 jit_solution(14238672206659687530)
XLA Ops:
  0.6 0.0 copy-start.7
  0.6 0.0 copy-start
  0.7 1.0 reduce-window.4
  1.6 0.7 fusion.29
  2.3 0.9 select_reduce_fusion
  3.1 0.3 fusion.25
  3.4 1.2 broadcast_in_dim.10
  4.6 1.6 %copy.28 = f32[512,512]{1,0:T(8,128)S(1)} copy(f32[512,512]{0,1:T(8,128)} %bitcast.63) | data formatting | bytes 2097152 | tf_op jit(solution)/shard_map/reshape | solution.py:366
  6.1 1.1 copy.25
  7.2 1.0 copy.26
  8.2 0.0 copy-done.7
  8.2 63.1 %shard_map.103 = (bf16[4096,1024]{1,0:T(8,128)(2,1)S(1)}, bf16[4096,512]{1,0:T(8,128)(2,1)S(1)}, bf16[1024,512]{1,0:T(8,128)(2,1)S(1)}) custom-call(bf16[512,1024]{1,0:T(8,128)(2,1)S(1)} %copy-done.7, bf16[256,512]{1,0:T(8,128)(2,1)S(1)} %bitcast.59, bf16[64,512]{1,0:T(8,128)(2,1)S(1)} %bitcast.60), custom_call_target="tpu_custom_call" | custom-call | tf_op jit(solution)/shard_map/pallas_call | solution.py:277
  71.4 0.0 copy-start.1
  71.4 3.2 %copy-done.1 = bf16[4096,1024]{1,0:T(8,128)(2,1)} copy-done((bf16[4096,1024]{1,0:T(8,128)(2,1)}, bf16[4096,1024]{1,0:T(8,128)(2,1)S(1)}, u32[]{:S(2)}) %copy-start.1) | copy-done | bytes 8388632
  74.6 0.0 copy-start.5
  74.6 2.0 %copy-done.5 = bf16[4096,512]{1,0:T(8,128)(2,1)} copy-done((bf16[4096,512]{1,0:T(8,128)(2,1)}, bf16[4096,512]{1,0:T(8,128)(2,1)S(1)}, u32[]{:S(2)}) %copy-start.5) | copy-done | bytes 4194328
  76.6 0.0 copy-done
  76.6 0.7 fusion.5.lora_ref
  77.4 0.1 fusion.24
  77.5 0.1 copy.29
  77.6 4.1 %fusion.down_ref = bf16[4096,128]{1,0:T(8,128)(2,1)S(1)} fusion(bf16[512,4096]{1,0:T(8,128)(2,1)} %param.8, f32[512,128]{1,0:T(8,128)S(1)} %copy.29, bf16[512,512]{1,0:T(8,128)(2,1)S(1)} %fusion.5.lora_ref, s32[128]{0:T(128)S(1)} %iota_and_fusion.2, s32[512]{0:T(512)S(1)} %iota_and_fusion.1), kind=kOutput, calls=%fused_computation.1 | convolution fusion | flops 604700672 | bytes 6031872 | tf_op jit(solution)/shard_map/dot_general | solution.py:324
  81.7 6.5 %fusion.9 = bf16[512,128]{1,0:T(8,128)(2,1)S(1)} fusion(f32[512,128]{1,0:T(8,128)S(1)} %copy.29, f32[512,512]{0,1:T(8,128)} %bitcast.64, bf16[4096,512]{1,0:T(8,128)(2,1)} %copy-done.5, bf16[512,4096]{1,0:T(8,128)(2,1)} %param.8, s32[128]{0:T(128)S(1)} %iota_and_fusion.2, s32[512]{0:T(512)S(1)} %iota_and_fusion.1), kind=kOutput, calls=%fused_computation.16 | convolution fusion | flops 2215313408 | bytes 9832960 | tf_op jit(solution)/shard_map/dot_general | solution.py:324
  88.2 0.6 fusion.7.up_ref
  88.7 0.1 iota_compare_fusion.2
  88.8 0.0 copy-start.2
  88.8 3.4 %copy-done.2 = bf16[4096,1024]{1,0:T(8,128)(2,1)S(1)} copy-done((bf16[4096,1024]{1,0:T(8,128)(2,1)S(1)}, bf16[4096,1024]{1,0:T(8,128)(2,1)}, u32[]{:S(2)}) %copy-start.2) | copy-done | bytes 8388632
  92.2 0.0 copy-start.6
  92.2 2.2 %copy-done.6 = bf16[4096,512]{1,0:T(8,128)(2,1)S(1)} copy-done((bf16[4096,512]{1,0:T(8,128)(2,1)S(1)}, bf16[4096,512]{1,0:T(8,128)(2,1)}, u32[]{:S(2)}) %copy-start.6) | copy-done | bytes 4194328
  94.4 33.8 %shard_map.104 = (bf16[256,2048]{1,0:T(8,128)(2,1)S(1)}, bf16[64,2048]{1,0:T(8,128)(2,1)S(1)}, bf16[16,16,128]{2,1,0:T(8,128)(2,1)S(1)}, bf16[512,4096]{1,0:T(8,128)(2,1)S(1)}) custom-call(bf16[4096,128]{1,0:T(8,128)(2,1)S(1)} %fusion.down_ref, bf16[1024,128]{1,0:T(8,128)(2,1)S(1)} %fusion.7.up_ref, bf16[16,128]{1,0:T(8,128)(2,1)S(1)} %pad_convert_fusion.hot_ref, ...), custom_call_target="tpu_custom_call" | custom-call | tf_op jit(solution)/shard_map/pallas_call | solution.py:277
  128.2 0.0 copy-start.3
  128.2 2.0 %copy-done.3 = bf16[512,4096]{1,0:T(8,128)(2,1)} copy-done((bf16[512,4096]{1,0:T(8,128)(2,1)}, bf16[512,4096]{1,0:T(8,128)(2,1)S(1)}, u32[]{:S(2)}) %copy-start.3) | copy-done | bytes 4194328
  130.3 0.0 copy-start.8
  130.3 1.0 copy-done.8
  131.2 0.0 copy-start.9
  131.2 0.1 broadcast_in_dim.12
  131.3 0.2 copy.33
  131.5 0.0 copy-start.4
  131.5 0.6 compare_select_fusion
  132.1 1.4 %fusion.15 = f32[32,16,64]{2,1,0:T(8,128)} fusion(bf16[32,16,2048]{2,1,0:T(8,128)(2,1)S(1)} %bitcast.61, bf16[64,2048]{1,0:T(8,128)(2,1)S(1)} %get-tuple-element.16), kind=kOutput, calls=%fused_computation.21 | convolution fusion | flops 134217728 | bytes 2490368 | tf_op jit(solution)/shard_map/dot_general | solution.py:324
  133.5 0.0 copy-done.9
  133.6 1.5 %fusion.10 = f32[32,16,256]{2,1,0:T(8,128)} fusion(bf16[32,16,2048]{2,1,0:T(8,128)(2,1)S(1)} %bitcast.62, bf16[256,2048]{1,0:T(8,128)(2,1)S(1)} %copy-done.9), kind=kOutput, calls=%fused_computation.17 | convolution fusion | flops 536870912 | bytes 3670016 | tf_op jit(solution)/shard_map/dot_general | solution.py:324
  135.1 0.0 copy-done.4
  135.1 2.0 %copy.38 = bf16[512,4096]{1,0:T(8,128)(2,1)} copy(bf16[512,4096]{1,0:T(8,128)(2,1)S(1)} %copy-done.4) | data formatting | bytes 8388608
  (6 shorter events, 0.0 us)
Async XLA Ops:
  0.6 7.6 %copy-start.7 = (bf16[512,1024]{1,0:T(8,128)(2,1)S(1)}, bf16[512,1024]{1,0:T(8,128)(2,1)}, u32[]{:S(2)}) copy-start(bf16[512,1024]{1,0:T(8,128)(2,1)} %weight_ref.1) | copy-start | bytes 3145732
  0.6 76.0 %copy-start = (bf16[512,1024]{1,0:T(8,128)(2,1)S(1)}, bf16[512,1024]{1,0:T(8,128)(2,1)}, u32[]{:S(2)}) copy-start(bf16[512,1024]{1,0:T(8,128)(2,1)} %grad_ref.1) | copy-start | bytes 3145732
  71.4 3.2 %copy-start.1 = (bf16[4096,1024]{1,0:T(8,128)(2,1)}, bf16[4096,1024]{1,0:T(8,128)(2,1)S(1)}, u32[]{:S(2)}) copy-start(bf16[4096,1024]{1,0:T(8,128)(2,1)S(1)} %get-tuple-element.12.weight_ref) | copy-start | bytes 25165828
  74.6 2.0 %copy-start.5 = (bf16[4096,512]{1,0:T(8,128)(2,1)}, bf16[4096,512]{1,0:T(8,128)(2,1)S(1)}, u32[]{:S(2)}) copy-start(bf16[4096,512]{1,0:T(8,128)(2,1)S(1)} %get-tuple-element.11.maps_ref) | copy-start | bytes 12582916
  88.8 3.4 %copy-start.2 = (bf16[4096,1024]{1,0:T(8,128)(2,1)S(1)}, bf16[4096,1024]{1,0:T(8,128)(2,1)}, u32[]{:S(2)}) copy-start(bf16[4096,1024]{1,0:T(8,128)(2,1)} %copy-done.1) | copy-start | bytes 25165828
  92.2 2.2 %copy-start.6 = (bf16[4096,512]{1,0:T(8,128)(2,1)S(1)}, bf16[4096,512]{1,0:T(8,128)(2,1)}, u32[]{:S(2)}) copy-start(bf16[4096,512]{1,0:T(8,128)(2,1)} %copy-done.5) | copy-start | bytes 12582916
  128.2 2.0 %copy-start.3 = (bf16[512,4096]{1,0:T(8,128)(2,1)}, bf16[512,4096]{1,0:T(8,128)(2,1)S(1)}, u32[]{:S(2)}) copy-start(bf16[512,4096]{1,0:T(8,128)(2,1)S(1)} %get-tuple-element.20) | copy-start | bytes 12582916
  130.3 1.0 copy-start.8
  131.2 2.3 %copy-start.9 = (bf16[256,2048]{1,0:T(8,128)(2,1)S(1)}, bf16[256,2048]{1,0:T(8,128)(2,1)}, u32[]{:S(2)}) copy-start(bf16[256,2048]{1,0:T(8,128)(2,1)} %copy-done.8) | copy-start | bytes 3145732
  131.5 3.6 %copy-start.4 = (bf16[512,4096]{1,0:T(8,128)(2,1)S(1)}, bf16[512,4096]{1,0:T(8,128)(2,1)}, u32[]{:S(2)}) copy-start(bf16[512,4096]{1,0:T(8,128)(2,1)} %copy-done.3) | copy-start | bytes 12582916

commit v5 on v4

--- a/solution.py
+++ b/solution.py
@@ -144,15 +144,17 @@
                         self.copies[i, way, step].wait_recv()
                 if step + 1 < self.steps:
                     self.send(i, step + 1)
-            for i, slot, device, start, count in self.arrived(step):
-                item = self.items[i]
-                block = self.target_rows(item, device, self.lane, start, count)
-                if item[3]:
-                    self.pair(i, block, slot)
-                self.side(i, block, device, start, count, slot)
-            if step:
-                self.cross(step - 1)
-        self.cross(self.steps - 1)
+                for which, slot, device, start, count in self.arrived(step):
+                    if which != i:
+                        continue
+                    block = self.target_rows(item, device, self.lane, start, count)
+                    if item[3]:
+                        self.pair(i, block, slot)
+                    self.side(i, block, device, start, count, slot)
+            if step >= 2:
+                self.cross(step - 2)
+        for step in range(max(self.steps - 2, 0), self.steps):
+            self.cross(step)
 
     def cross(self, step):
         for i, slot, device, start, count in self.arrived(step):
@@ -281,7 +283,7 @@
         out_specs=[anywhere] * len(outs),
         scratch_shapes=scratch,
         compiler_params=pltpu.CompilerParams(
-            collective_id=collective_id, has_side_effects=True, vmem_limit_bytes=32 * 1024 * 1024
+            collective_id=collective_id, has_side_effects=True, vmem_limit_bytes=56 * 1024 * 1024
         ),
     )(*operands)
 

time: 137 us -> 125 us (0.912)
  local copies, waits for them, and re-layouts: 21 us -> 9.36 us
  Pallas kernels: 97 us -> 91.3 us
  matrix products: 15 us -> 19.2 us
    unnamed x21 -> x11, local copies, waits for them, and re-layouts: 15.8 us -> 2.04 us
    pallas_call x2, Pallas kernels: 97 us -> 91.3 us  [call(): pl.pallas_call(kernel, out_shape=outs, in_specs=[anywhere] * len(operands...]
    dot_general x7, matrix products: 15 us -> 19.2 us  [dot(): lax.dot_general(left, right, (((left_dim,), (right_dim,)), ((), ())), pre...]
where the time goes in v5:
time: 125 us; the launch traced here: 124 us
  Pallas kernels  91.3 us (73%)
  matrix products  19.2 us (15%)
  local copies, waits for them, and re-layouts  9.36 us (7%)
  other arithmetic  3.81 us (3%)
    pallas_call x2, Pallas kernels, call(): pl.pallas_call(kernel, out_shape=outs, in_specs=[anywhere] * len(operands...  91.3 us
    dot_general x7, matrix products, dot(): lax.dot_general(left, right, (((left_dim,), (right_dim,)), ((), ())), pre...  19.2 us

profile of v5, /device:TPU:13, one launch (start us, length us, event | category | flops | bytes accessed | tf_op | source)
XLA Modules:
  0.0 124.4 jit_solution(8506520445507167010)
XLA Ops:
  0.6 0.0 copy-start
  0.6 0.9 reduce-window.4
  1.6 0.7 fusion.29
  2.2 0.9 select_reduce_fusion
  3.1 0.3 fusion.25
  3.3 1.1 broadcast_in_dim.10
  4.4 1.6 %copy.28 = f32[512,512]{1,0:T(8,128)S(1)} copy(f32[512,512]{0,1:T(8,128)} %bitcast.61) | data formatting | bytes 2097152 | tf_op jit(solution)/shard_map/reshape | solution.py:368
  6.0 1.8 %copy.25 = bf16[512,256]{0,1:T(8,128)(2,1)} copy(bf16[512,256]{1,0:T(8,128)(2,1)} %bitcast.66) | data formatting | bytes 524288 | tf_op jit(solution)/shard_map/reshape | solution.py:350
  7.8 1.6 %copy.26 = bf16[512,64]{0,1:T(8,128)(2,1)} copy(bf16[512,64]{1,0:T(8,128)(2,1)} %bitcast.68) | data formatting | bytes 131072 | tf_op jit(solution)/shard_map/reshape | solution.py:351
  9.4 57.1 %shard_map.103 = (bf16[4096,1024]{1,0:T(8,128)(2,1)}, bf16[4096,512]{1,0:T(8,128)(2,1)}, bf16[1024,512]{1,0:T(8,128)(2,1)}) custom-call(bf16[512,1024]{1,0:T(8,128)(2,1)} %weight_ref.1, bf16[256,512]{1,0:T(8,128)(2,1)} %bitcast.65, bf16[64,512]{1,0:T(8,128)(2,1)} %bitcast.67), custom_call_target="tpu_custom_call" | custom-call | tf_op jit(solution)/shard_map/pallas_call | solution.py:279
  66.5 0.0 copy-done
  66.5 1.9 %fusion.5.lora_ref = bf16[512,512]{1,0:T(8,128)(2,1)S(1)} fusion(f32[512,512]{1,0:T(8,128)S(1)} %copy.28, bf16[512,1024]{1,0:T(8,128)(2,1)S(1)} %copy-done, bf16[1024,512]{1,0:T(8,128)(2,1)} %get-tuple-element.10), kind=kOutput, calls=%fused_computation.9 | convolution fusion | flops 537657344 | bytes 3670016 | tf_op jit(solution)/shard_map/dot_general | solution.py:326
  68.4 0.0 copy-start.1
  68.5 0.0 copy-start.3
  68.5 0.1 fusion.24
  68.6 0.1 copy.29
  68.7 5.3 %fusion.down_ref = bf16[4096,128]{1,0:T(8,128)(2,1)} fusion(bf16[512,4096]{1,0:T(8,128)(2,1)} %param.8, f32[512,128]{1,0:T(8,128)S(1)} %copy.29, bf16[512,512]{1,0:T(8,128)(2,1)S(1)} %fusion.5.lora_ref, s32[128]{0:T(128)S(1)} %iota_and_fusion.2, s32[512]{0:T(512)S(1)} %iota_and_fusion.1), kind=kOutput, calls=%fused_computation.1 | convolution fusion | flops 604700672 | bytes 6031872 | tf_op jit(solution)/shard_map/dot_general | solution.py:326
  74.0 0.0 copy-done.3
  74.0 6.3 %fusion.9 = bf16[512,128]{1,0:T(8,128)(2,1)S(1)} fusion(f32[512,128]{1,0:T(8,128)S(1)} %copy.29, f32[512,512]{0,1:T(8,128)S(1)} %bitcast.62, bf16[4096,512]{1,0:T(8,128)(2,1)} %get-tuple-element.11.maps_ref, bf16[512,4096]{1,0:T(8,128)(2,1)} %param.8, s32[128]{0:T(128)S(1)} %iota_and_fusion.2, s32[512]{0:T(512)S(1)} %iota_and_fusion.1), kind=kOutput, calls=%fused_computation.16 | convolution fusion | flops 2215313408 | bytes 9832960 | tf_op jit(solution)/shard_map/dot_general | solution.py:326
  80.3 0.0 copy-done.1
  80.3 1.3 %fusion.7.up_ref = bf16[1024,128]{1,0:T(8,128)(2,1)} fusion(bf16[512,128]{1,0:T(8,128)(2,1)S(1)} %fusion.9, bf16[512,1024]{1,0:T(8,128)(2,1)S(1)} %copy-done), kind=kOutput, calls=%fused_computation.14 | convolution fusion | flops 134479872 | bytes 1441792 | tf_op jit(solution)/shard_map/dot_general | solution.py:326
  81.6 0.1 iota_compare_fusion.2
  81.6 0.6 pad_convert_fusion.hot_ref
  82.2 34.2 %shard_map.104 = (bf16[256,2048]{1,0:T(8,128)(2,1)}, bf16[64,2048]{1,0:T(8,128)(2,1)}, bf16[16,16,128]{2,1,0:T(8,128)(2,1)}, bf16[512,4096]{1,0:T(8,128)(2,1)}) custom-call(bf16[4096,128]{1,0:T(8,128)(2,1)} %fusion.down_ref, bf16[1024,128]{1,0:T(8,128)(2,1)} %fusion.7.up_ref, bf16[16,128]{1,0:T(8,128)(2,1)} %pad_convert_fusion.hot_ref, ...), custom_call_target="tpu_custom_call" | custom-call | tf_op jit(solution)/shard_map/pallas_call | solution.py:279
  116.5 0.0 copy-start.4
  116.5 0.8 slice_bitcast_fusion
  117.3 0.1 broadcast_in_dim.12
  117.4 0.2 copy.33
  117.6 0.0 copy-start.2
  117.6 0.6 compare_select_fusion
  118.2 2.7 %fusion.15 = f32[32,16,64]{2,1,0:T(8,128)} fusion(bf16[32,16,2048]{2,1,0:T(8,128)(2,1)S(1)} %bitcast.59, bf16[64,2048]{1,0:T(8,128)(2,1)} %get-tuple-element.16), kind=kOutput, calls=%fused_computation.21 | convolution fusion | flops 134217728 | bytes 2490368 | tf_op jit(solution)/shard_map/dot_general | solution.py:326
  120.9 0.0 copy-done.4
  120.9 1.5 %fusion.10 = f32[32,16,256]{2,1,0:T(8,128)} fusion(bf16[32,16,2048]{2,1,0:T(8,128)(2,1)S(1)} %bitcast.60, bf16[256,2048]{1,0:T(8,128)(2,1)S(1)} %copy-done.4), kind=kOutput, calls=%fused_computation.17 | convolution fusion | flops 536870912 | bytes 3670016 | tf_op jit(solution)/shard_map/dot_general | solution.py:326
  122.4 0.0 copy-done.2
  122.4 2.0 %copy.38 = bf16[512,4096]{1,0:T(8,128)(2,1)} copy(bf16[512,4096]{1,0:T(8,128)(2,1)S(1)} %copy-done.2) | data formatting | bytes 8388608
  (4 shorter events, 0.0 us)
Async XLA Ops:
  0.6 65.9 %copy-start = (bf16[512,1024]{1,0:T(8,128)(2,1)S(1)}, bf16[512,1024]{1,0:T(8,128)(2,1)}, u32[]{:S(2)}) copy-start(bf16[512,1024]{1,0:T(8,128)(2,1)} %grad_ref.1) | copy-start | bytes 3145732
  68.4 11.8 %copy-start.1 = (bf16[512,512]{1,0:T(8,128)(2,1)}, bf16[512,512]{1,0:T(8,128)(2,1)S(1)}, u32[]{:S(2)}) copy-start(bf16[512,512]{1,0:T(8,128)(2,1)S(1)} %fusion.5.lora_ref) | copy-start | bytes 1572868
  68.5 5.6 %copy-start.3 = (f32[512,32,16]{0,2,1:T(8,128)S(1)}, f32[512,32,16]{0,2,1:T(8,128)}, u32[]{:S(2)}) copy-start(f32[512,32,16]{0,2,1:T(8,128)} %broadcast_in_dim.10) | copy-start | bytes 3145732
  116.5 4.4 %copy-start.4 = (bf16[256,2048]{1,0:T(8,128)(2,1)S(1)}, bf16[256,2048]{1,0:T(8,128)(2,1)}, u32[]{:S(2)}) copy-start(bf16[256,2048]{1,0:T(8,128)(2,1)} %get-tuple-element.15) | copy-start | bytes 3145732
  117.6 4.8 %copy-start.2 = (bf16[512,4096]{1,0:T(8,128)(2,1)S(1)}, bf16[512,4096]{1,0:T(8,128)(2,1)}, u32[]{:S(2)}) copy-start(bf16[512,4096]{1,0:T(8,128)(2,1)} %get-tuple-element.20) | copy-start | bytes 12582916
